TPU v7x, 32 devices: a whole 2x2x4 slice. The times are simulated.
32 devices in a mesh: az: 4 (over z), rg: 8 (over y, x, core).
Axes of the slice: x: 2, y: 2, z: 4, core: 2. Of those that a mesh axis runs over, the one named last changes fastest.
Arguments:
- echo_planes: float32 [2, 4096, 8192], P(None, 'rg', 'az'), may hold values from -6 to 6
- pulse_phase: float32 [384], replicated, may hold values from -3.140625 to 3.140625
- band_offsets: int32 [4, 4, 8], P(None, 'az', 'rg'), may hold values from 0 to 57, as said below
- band_weights: float32 [4, 4, 8, 4096], P(None, 'az', None, 'rg'), may hold values from -2 to 2
- azimuth_rate: float32 [4096], P('rg'), may hold values from 16 to 256
Outputs:
- focused: float32 [2, 4096, 8192], P(None, 'rg', 'az')
Inputs may be any that keep to these rules, and one draw needn't show every extreme that they name: band_offsets[b, j, r] counts rows from a bin's own row; the value 57 occurs in every draw.
All inputs are finite; a program needn't handle non-finite values.
Results may differ from a plain program's by a relative error of at most 0.004.
Values may be sent and summed in bfloat16 or wider, within the bound.
A program may use at most 192 MiB of HBM per device.

v0:
```python
import math

import jax
import jax.numpy as jnp
from jax import lax
from jax.sharding import PartitionSpec as P

RIM_ROWS = 64


precise = lax.Precision.HIGHEST


def passed_along(value, axis, steps):
    count = lax.axis_size(axis)
    initial, last = (max(0, -steps), min(count, count - steps))
    return lax.ppermute(value, axis, [(source, source + steps) for source in range(initial, last)])


def angle_pair(product, period):
    angles = 2.0 * math.pi / period * (product % period).astype(jnp.float32)
    return (jnp.cos(angles), jnp.sin(angles))


def complex_contract(real_in, imag_in, cos_table, sin_table, orient, pattern):
    real_out = jnp.einsum(pattern, real_in, cos_table, precision=precise) - orient * jnp.einsum(
        pattern, imag_in, sin_table, precision=precise
    )
    imag_out = jnp.einsum(pattern, imag_in, cos_table, precision=precise) + orient * jnp.einsum(
        pattern, real_in, sin_table, precision=precise
    )
    return (real_out, imag_out)


def local_transform(real_in, imag_in, orient, factor):
    length = real_in.shape[-1]
    leading = real_in.shape[:-1]
    first_size = 8
    second_size = length // first_size
    real_in = real_in.reshape(leading + (first_size, second_size))
    imag_in = imag_in.reshape(leading + (first_size, second_size))
    index_one = jnp.arange(first_size, dtype=jnp.int32)
    index_two = jnp.arange(second_size, dtype=jnp.int32)
    cos_one, sin_one = angle_pair(index_one[:, None] * index_one[None, :], first_size)
    section_real, section_imag = complex_contract(
        real_in, imag_in, cos_one, sin_one, orient, "...ab,ak->...kb"
    )
    twist_cos, twist_sin = angle_pair(index_one[:, None] * index_two[None, :], length)
    turned_real = section_real * twist_cos - orient * section_imag * twist_sin
    turned_imag = section_imag * twist_cos + orient * section_real * twist_sin
    cos_two, sin_two = angle_pair(index_two[:, None] * index_two[None, :], second_size)
    final_real, final_imag = complex_contract(
        turned_real, turned_imag, cos_two, sin_two, orient, "...kb,bj->...jk"
    )
    return (
        final_real.reshape(leading + (length,)) * factor,
        final_imag.reshape(leading + (length,)) * factor,
    )


def make_band(values, tile_rows, window_rows):
    padded = jnp.concatenate([values, jnp.zeros((tile_rows,), jnp.float32)])
    repeated = jnp.tile(padded, tile_rows)[: tile_rows * window_rows]
    return repeated.reshape(tile_rows, window_rows)


def compress(extended, out_rows, phases):
    code_length = phases.shape[0]
    tile_rows = math.gcd(out_rows, 128)
    window_rows = tile_rows + code_length - 1
    norm_scale = 1.0 / math.sqrt(code_length)
    band_cos = make_band(jnp.cos(phases) * norm_scale, tile_rows, window_rows)
    band_sin = make_band(jnp.sin(phases) * norm_scale, tile_rows, window_rows)
    block_table = jnp.concatenate(
        [
            jnp.concatenate([band_cos, band_sin], axis=1),
            jnp.concatenate([-band_sin, band_cos], axis=1),
        ],
        axis=0,
    )
    pieces = []
    for tile_index in range(out_rows // tile_rows):
        window = extended[:, tile_index * tile_rows : tile_index * tile_rows + window_rows, :]
        window = window.reshape(2 * window_rows, extended.shape[2])
        product = jnp.dot(
            block_table, window, precision=precise, preferred_element_type=jnp.float32
        )
        pieces.append(product.reshape(2, tile_rows, extended.shape[2]))
    return jnp.concatenate(pieces, axis=1)


def local(echo_planes, pulse_phase, band_offsets, band_weights, azimuth_rate):
    bank_count = lax.axis_size("az")
    bank_index = lax.axis_index("az")
    row_count = echo_planes.shape[1]
    pulse_local = echo_planes.shape[2]
    pulse_count = pulse_local * bank_count
    bin_group = pulse_local // bank_count
    tap_count = band_weights.shape[2]
    code_length = pulse_phase.shape[0]
    echo_rim = passed_along(echo_planes[:, : code_length - 1, :], "rg", -1)
    extended = jnp.concatenate([echo_planes, echo_rim], axis=1)
    compressed = compress(extended, row_count, pulse_phase)
    spec_real, spec_imag = local_transform(compressed[0], compressed[1], -1, 1.0)
    bin_index = jnp.arange(pulse_local, dtype=jnp.int32)
    twist_cos, twist_sin = angle_pair(bank_index * bin_index, pulse_count)
    partial_real = spec_real * twist_cos + spec_imag * twist_sin
    partial_imag = spec_imag * twist_cos - spec_real * twist_sin
    partial_value = jnp.stack([partial_real, partial_imag]).astype(jnp.bfloat16)
    received = lax.all_to_all(partial_value[None], "az", split_axis=3, concat_axis=0, tiled=True)
    source_count = received.shape[0]
    source_ids = jnp.arange(source_count, dtype=jnp.int32)
    fold_cos, fold_sin = angle_pair(source_ids[:, None] * source_ids[None, :], source_count)
    recv_real = received[:, 0].astype(jnp.float32)
    recv_imag = received[:, 1].astype(jnp.float32)
    out_real, out_imag = complex_contract(
        recv_real, recv_imag, fold_cos, fold_sin, -1, "ark,ab->rbk"
    )
    spectrum = jnp.stack([out_real, out_imag])
    doppler_edge = passed_along(spectrum[:, :RIM_ROWS].astype(jnp.bfloat16), "rg", -1).astype(
        jnp.float32
    )
    widened = jnp.concatenate([spectrum, doppler_edge], axis=1)
    migrated_list = []
    for group_index in range(bank_count):
        slab = lax.dynamic_slice_in_dim(
            widened[:, :, group_index, :],
            band_offsets[group_index, 0, 0],
            row_count + tap_count - 1,
            axis=1,
        )
        accum = jnp.zeros((2, row_count, bin_group), jnp.float32)
        for tap_index in range(tap_count):
            accum = (
                accum
                + band_weights[group_index, 0, tap_index][None, :, None]
                * slab[:, tap_index : tap_index + row_count, :]
            )
        migrated_list.append(accum)
    migrated = jnp.stack(migrated_list, axis=2)
    bank_ids = jnp.arange(bank_count, dtype=jnp.int32)
    local_bins = bank_index * bin_group + jnp.arange(bin_group, dtype=jnp.int32)
    doppler_bin = local_bins[None, :] + pulse_local * bank_ids[:, None]
    centered = jnp.where(doppler_bin < pulse_count // 2, doppler_bin, doppler_bin - pulse_count)
    doppler_freq = centered.astype(jnp.float32) / pulse_count
    base_phase = jnp.pi * doppler_freq * doppler_freq
    phases = base_phase[None, :, :] * azimuth_rate[:, None, None]
    phase_cos = jnp.cos(phases)
    phase_sin = jnp.sin(phases)
    filtered_real = migrated[0] * phase_cos - migrated[1] * phase_sin
    filtered_imag = migrated[0] * phase_sin + migrated[1] * phase_cos
    fold_cos, fold_sin = angle_pair(bank_ids[:, None] * bank_ids[None, :], bank_count)
    sum_real, sum_imag = complex_contract(
        filtered_real, filtered_imag, fold_cos, fold_sin, 1, "rbk,ba->ark"
    )
    sum_real = sum_real * (1.0 / bank_count)
    sum_imag = sum_imag * (1.0 / bank_count)
    back_cos, back_sin = angle_pair(bank_ids[:, None] * local_bins[None, :], pulse_count)
    folded_real = sum_real * back_cos[:, None, :] - sum_imag * back_sin[:, None, :]
    folded_imag = sum_imag * back_cos[:, None, :] + sum_real * back_sin[:, None, :]
    folded = jnp.stack([folded_real, folded_imag], axis=1).astype(jnp.bfloat16)
    received = lax.all_to_all(folded, "az", split_axis=0, concat_axis=3, tiled=True)
    recv_real = received[0, 0].astype(jnp.float32)
    recv_imag = received[0, 1].astype(jnp.float32)
    out_real, out_imag = local_transform(recv_real, recv_imag, 1, 1.0 / recv_real.shape[-1])
    return jnp.stack([out_real, out_imag])


def solution(mesh):
    in_specs = (P(None, "rg", "az"), P(), P(None, "az", "rg"), P(None, "az", None, "rg"), P("rg"))
    out_specs = P(None, "rg", "az")
    return jax.shard_map(local, mesh=mesh, in_specs=in_specs, out_specs=out_specs, check_vma=False)
```

profile of v0, /device:TPU:4, one launch (start us, length us, event | category | flops | bytes accessed | tf_op | source)
XLA Modules:
  0.0 634.6 jit_solution(12013427738562261185)
XLA Ops:
  0.0 6.3 slice.271
  10.1 7.6 %reshape.495 = f32[1022,2048,1]{1,0,2:T(8,128)} reshape(f32[2,511,2048]{2,1,0:T(8,128)} %bitcast.249) | data formatting | bytes 16744448 | tf_op jit(solution)/shard_map/reshape | solution.py:84
  18.1 8.0 %constant_dynamic-update-slice_fusion.1 = f32[2,895,2048]{2,1,0:T(8,128)} fusion(f32[2,512,2048]{2,1,0:T(8,128)} %param.5), kind=kLoop, calls=%fused_computation.198 | loop fusion | bytes 16777216
  26.1 7.3 %fusion.291 = f32[2,128,2048]{2,1,0:T(8,128)S(1)} fusion(f32[2,128,1022]{2,1,0:T(8,128)S(1)} %bitcast.260, f32[1022,2048,1]{1,0,2:T(8,128)S(1)} %bitcast.259), kind=kOutput, calls=%fused_computation.354 | convolution fusion | flops 6429868032 | bytes 11515904 | tf_op jit(solution)/shard_map/dot_general | solution.py:85
  33.4 44.5 %collective-permute-done = f32[2,383,2048]{2,1,0:T(8,128)} collective-permute-done((f32[2,383,2048]{2,1,0:T(8,128)}, f32[2,383,2048]{2,1,0:T(8,128)}, u32[]{:S(2)}, u32[]{:S(2)}) %collective-permute-start) | collective-permute-done | bytes 6275104 | tf_op jit(solution)/shard_map/ppermute | solution.py:17
  77.9 6.3 constant_dynamic-update-slice_fusion
  84.1 17.9 %fusion.276 = (f32[2,511,2048]{2,1,0:T(8,128)}, f32[2,511,2048]{2,1,0:T(8,128)}, f32[2,511,2048]{2,1,0:T(8,128)}) fusion(f32[2,895,2048]{2,1,0:T(8,128)} %constant_dynamic-update-slice_fusion), kind=kLoop, calls=%fused_computation.347 | loop fusion | bytes 50233344 | tf_op jit(solution)/shard_map/slice | solution.py:83
  102.0 7.5 %reshape.496 = f32[1022,2048,1]{1,0,2:T(8,128)} reshape(f32[2,511,2048]{2,1,0:T(8,128)} %get-tuple-element.5) | data formatting | bytes 16744448 | tf_op jit(solution)/shard_map/reshape | solution.py:84
  109.5 10.5 %fusion.292 = f32[2,128,2048]{2,1,0:T(8,128)} fusion(f32[2,128,1022]{2,1,0:T(8,128)S(1)} %bitcast.261, f32[1022,2048,1]{1,0,2:T(8,128)} %reshape.496), kind=kOutput, calls=%fused_computation.355 | convolution fusion | flops 6429868032 | bytes 11515904 | tf_op jit(solution)/shard_map/dot_general | solution.py:85
  120.0 7.6 %reshape.497 = f32[1022,2048,1]{1,0,2:T(8,128)} reshape(f32[2,511,2048]{2,1,0:T(8,128)} %get-tuple-element.7) | data formatting | bytes 16744448 | tf_op jit(solution)/shard_map/reshape | solution.py:84
  127.6 10.6 %fusion.293 = f32[2,128,2048]{2,1,0:T(8,128)} fusion(f32[2,128,1022]{2,1,0:T(8,128)S(1)} %bitcast.262, f32[1022,2048,1]{1,0,2:T(8,128)} %reshape.497), kind=kOutput, calls=%fused_computation.356 | convolution fusion | flops 6429868032 | bytes 11515904 | tf_op jit(solution)/shard_map/dot_general | solution.py:85
  138.2 7.6 %reshape.498 = f32[1022,2048,1]{1,0,2:T(8,128)} reshape(f32[2,511,2048]{2,1,0:T(8,128)} %get-tuple-element.6) | data formatting | bytes 16744448 | tf_op jit(solution)/shard_map/reshape | solution.py:84
  145.8 9.8 %fusion.294 = f32[2,128,2048]{2,1,0:T(8,128)S(1)} fusion(f32[2,128,1022]{2,1,0:T(8,128)S(1)} %bitcast.263, f32[1022,2048,1]{1,0,2:T(8,128)} %reshape.498), kind=kOutput, calls=%fused_computation.357 | convolution fusion | flops 6429868032 | bytes 11515904 | tf_op jit(solution)/shard_map/dot_general | solution.py:85
  179.3 6.2 fusion.20
  185.6 6.0 fusion.18
  191.5 6.5 %subtract_bitcast_fusion.2 = f32[512,256,8]{0,1,2:T(8,128)S(1)} fusion(f32[256,512,8]{1,0,2:T(8,128)S(1)} %fusion.20, f32[512,8,256]{2,1,0:T(8,128)S(1)} %get-tuple-element.18), kind=kOutput, calls=%fused_computation.35 | convolution fusion | flops 3224240128 | bytes 12582912 | tf_op jit(solution)/shard_map/...kb,bj->...jk/dot_general | solution.py:26
  198.0 6.4 %add_bitcast_fusion.2 = f32[512,256,8]{0,1,2:T(8,128)S(1)} fusion(f32[256,512,8]{1,0,2:T(8,128)S(1)} %fusion.18, f32[512,8,256]{2,1,0:T(8,128)S(1)} %get-tuple-element.18), kind=kOutput, calls=%fused_computation.34 | convolution fusion | flops 3224240128 | bytes 12582912 | tf_op jit(solution)/shard_map/...kb,bj->...jk/dot_general | solution.py:29
  209.4 19.2 %copy.60 = bf16[1,2,512,2048]{2,1,0,3:T(2,128)(2,1)} copy(bf16[1,2,512,2048]{2,3,1,0:T(8,128)(2,1)S(1)} %pad_maximum_fusion.4) | data formatting | bytes 8388608 | tf_op jit(solution)/shard_map/stack | solution.py:109
  233.5 94.4 %all-to-all-done = bf16[1,2,512,2048]{2,1,0,3:T(2,128)(2,1)} async-done(((bf16[1,2,512,2048]{2,1,0,3:T(2,128)(2,1)}), bf16[1,2,512,2048]{2,1,0,3:T(2,128)(2,1)}, u32[]{:S(2)}, u32[]{:S(2)}) %all-to-all-start) | async-done | bytes 4194336 | tf_op jit(solution)/shard_map/all_to_all | solution.py:110
  328.0 11.8 %copy.78 = bf16[1,2,512,4,512]{4,3,2,1,0:T(4,128)(2,1)} copy(bf16[1,2,512,4,512]{2,1,4,3,0:T(2,128)(2,1)} %bitcast.15) | data formatting | bytes 8388608 | tf_op jit(solution)/shard_map/all_to_all | solution.py:110
  376.3 7.0 %fusion.277 = (f32[2,576,1,512]{3,2,1,0:T(1,128)S(1)}, f32[2,576,1,512]{3,2,1,0:T(1,128)S(1)}, f32[2,576,1,512]{3,2,1,0:T(1,128)S(1)}, f32[2,576,1,512]{3,2,1,0:T(1,128)S(1)}) fusion(f32[2,576,4,512]{3,2,1,0:T(4,128)S(1)} %pad_maximum_fusion), kind=kLoop, calls=%fused_computation.348 | loop fusion | bytes 18874368 | tf_op jit(solution)/shard_map/slice | solution.py:127
  400.9 16.0 %fusion.4 = (f32[512,4,512]{2,0,1:T(8,128)S(1)}, f32[512,4,512]{2,0,1:T(8,128)S(1)}) fusion(f32[2,512,4,512]{3,1,0,2:T(8,128)S(1)} %pad_maximum_fusion.2, f32[512]{0:T(512)S(1)} %copy-done.10, f32[4,512]{1,0:T(4,128)S(1)} %get-tuple-element.60), kind=kLoop, calls=%fused_computation.10 | loop fusion | flops 7340032 | bytes 16787456 | tf_op jit(solution)/shard_map/sub | solution.py:150
  416.9 9.1 %fusion.28 = f32[4,512,512]{2,0,1:T(4,128)S(1)} fusion(f32[512,4,512]{2,0,1:T(8,128)S(1)} %get-tuple-element.21), kind=kOutput, calls=%fused_computation.58 | convolution fusion | flops 50331872 | bytes 8388608 | tf_op jit(solution)/shard_map/rbk,ba->ark/dot_general | solution.py:26
  425.9 9.3 %fusion.26 = f32[4,512,512]{2,0,1:T(4,128)S(1)} fusion(f32[512,4,512]{2,0,1:T(8,128)S(1)} %get-tuple-element.21), kind=kOutput, calls=%fused_computation.56 | convolution fusion | flops 50331872 | bytes 8388608 | tf_op jit(solution)/shard_map/rbk,ba->ark/dot_general | solution.py:29
  435.2 9.8 %fusion.34 = f32[4,512,512]{2,0,1:T(4,128)S(1)} fusion(f32[4,512,512]{2,0,1:T(4,128)S(1)} %fusion.28, f32[512,4,512]{2,0,1:T(8,128)S(1)} %get-tuple-element.20), kind=kOutput, calls=%fused_computation.64 | convolution fusion | flops 51380448 | bytes 12582912 | tf_op jit(solution)/shard_map/rbk,ba->ark/dot_general | solution.py:26
  445.0 12.1 %fusion.48 = (bf16[4,1,512,512]{3,0,2,1:T(4,128)(2,1)S(1)}, bf16[4,1,512,512]{3,0,2,1:T(4,128)(2,1)S(1)}) fusion(f32[4,512,512]{2,0,1:T(4,128)S(1)} %fusion.34, f32[4,512]{1,0:T(4,128)S(1)} %get-tuple-element.59, f32[4,512]{1,0:T(4,128)S(1)} %get-tuple-element.58, f32[4,512,512]{2,0,1:T(4,128)S(1)} %fusion.26, f32[512,4,512]{2,0,1:T(8,128)S(1)} %get-tuple-element.20), kind=kOutput, calls=%fused_computation.72 | convolution fusion | flops 59769056 | bytes 16793600 | tf_op jit(solution)/shard_map/rbk,ba->ark/dot_general | solution.py:29
  467.8 94.0 %all-to-all-done.1 = bf16[4,2,512,512]{3,2,1,0:T(8,128)(2,1)} async-done(((bf16[4,2,512,512]{3,2,1,0:T(8,128)(2,1)}), bf16[4,2,512,512]{3,2,1,0:T(8,128)(2,1)}, u32[]{:S(2)}, u32[]{:S(2)}) %all-to-all-start.1) | async-done | bytes 4194336 | tf_op jit(solution)/shard_map/all_to_all | solution.py:162
  561.9 7.3 %copy.68 = bf16[4,2,512,512]{2,3,0,1:T(8,128)(2,1)} copy(bf16[4,2,512,512]{3,2,1,0:T(8,128)(2,1)} %all-to-all-done.1) | data formatting | bytes 8388608 | tf_op jit(solution)/shard_map/all_to_all | solution.py:162
  591.9 6.2 fusion.12
  603.8 6.4 %multiply_bitcast_fusion.1 = f32[512,256,8]{0,1,2:T(8,128)S(1)} fusion(f32[256,512,8]{1,0,2:T(8,128)S(1)} %fusion.12, f32[512,8,256]{2,1,0:T(8,128)S(1)} %get-tuple-element.12), kind=kOutput, calls=%fused_computation.27 | convolution fusion | flops 3224240128 | bytes 12582912 | tf_op jit(solution)/shard_map/...kb,bj->...jk/dot_general | solution.py:26
  612.8 6.3 multiply_bitcast_fusion
  625.7 8.7 %copy.77 = f32[2,512,2048]{2,1,0:T(8,128)} copy(f32[2,512,2048]{1,2,0:T(8,128)} %pad_maximum_fusion.3) | data formatting | bytes 16777216 | tf_op jit(solution)/shard_map/stack | solution.py:166
  (97 shorter events, 132.0 us)
Async XLA Ops:
  0.0 9.1 %copy-start.11 = (f32[384]{0:T(512)S(1)}, f32[384]{0:T(512)}, u32[]{:S(2)}) copy-start(f32[384]{0:T(512)} %param.6) | copy-start | bytes 4612
  6.3 71.6 %collective-permute-start = (f32[2,383,2048]{2,1,0:T(8,128)}, f32[2,383,2048]{2,1,0:T(8,128)}, u32[]{:S(2)}, u32[]{:S(2)}) collective-permute-start(f32[2,383,2048]{2,1,0:T(8,128)} %slice.271), channel_id=1, source_target_pairs={{1,0},{2,1},{3,2},{4,3},{5,4},{6,5},{7,6},{9,8},{10,9},{11,10},{12... | collective-permute-start | bytes 18825224 | tf_op jit(solution)/shard_map/ppermute | solution.py:17
  17.8 8.3 %slice-start = ((s8[8388608]{0:T(1024)(128)(4,1)}), s8[4194304]{0:T(1024)(128)(4,1)S(1)}, s32[]{:S(2)}) async-start(s8[8388608]{0:T(1024)(128)(4,1)} %bitcast.258), calls=%async_computation.2 | async-start | bytes 8388608
  18.0 8.0 %slice-start.1 = ((s8[8388608]{0:T(1024)(128)(4,1)}), s8[4194304]{0:T(1024)(128)(4,1)S(1)}, s32[]{:S(2)}) async-start(s8[8388608]{0:T(1024)(128)(4,1)} %bitcast.258), calls=%async_computation.3 | async-start | bytes 8388608
  145.8 9.8 %copy-start.6 = (f32[2,128,2048]{2,1,0:T(8,128)S(1)}, f32[2,128,2048]{2,1,0:T(8,128)}, u32[]{:S(2)}) copy-start(f32[2,128,2048]{2,1,0:T(8,128)} %fusion.292) | copy-start | bytes 6291460
  145.8 9.8 %copy-start.7 = (f32[2,128,2048]{2,1,0:T(8,128)S(1)}, f32[2,128,2048]{2,1,0:T(8,128)}, u32[]{:S(2)}) copy-start(f32[2,128,2048]{2,1,0:T(8,128)} %fusion.293) | copy-start | bytes 6291460
  228.6 99.4 %all-to-all-start = ((bf16[1,2,512,2048]{2,1,0,3:T(2,128)(2,1)}), bf16[1,2,512,2048]{2,1,0,3:T(2,128)(2,1)}, u32[]{:S(2)}, u32[]{:S(2)}) async-start(bf16[1,2,512,2048]{2,1,0,3:T(2,128)(2,1)} %copy.60), calls=%async_computation | async-start | bytes 8388608 | tf_op jit(solution)/shard_map/all_to_all | solution.py:110
  339.8 5.2 copy-start
  353.4 4.7 copy-start.1
  358.1 2.0 copy-start.2
  358.1 4.0 copy-start.9
  358.1 12.6 %copy-start.8 = (f32[4,1,8,512]{3,2,1,0:T(8,128)S(1)}, f32[4,1,8,512]{3,2,1,0:T(8,128)}, u32[]{:S(2)}) copy-start(f32[4,1,8,512]{3,2,1,0:T(8,128)} %param.8) | copy-start | bytes 196612
  360.1 10.7 %collective-permute-start.1 = (bf16[2,64,4,512]{3,2,1,0:T(4,128)(2,1)S(1)}, bf16[2,64,4,512]{3,2,1,0:T(4,128)(2,1)S(1)}, u32[]{:S(2)}, u32[]{:S(2)}) collective-permute-start(bf16[2,64,4,512]{3,2,1,0:T(4,128)(2,1)S(1)} %fusion.86), channel_id=1, source_target_pairs={{1,0},{2,1},{3,2},{4,3},{5,4},{6,5},{7,6},{9,8},{10,9},{11,10},{12... | collective-permute-start | bytes 1572872 | tf_op jit(solution)/shard_map/ppermute | solution.py:17
  399.9 1.0 copy-start.10
  462.9 98.9 %all-to-all-start.1 = ((bf16[4,2,512,512]{3,2,1,0:T(8,128)(2,1)}), bf16[4,2,512,512]{3,2,1,0:T(8,128)(2,1)}, u32[]{:S(2)}, u32[]{:S(2)}) async-start(bf16[4,2,512,512]{3,2,1,0:T(8,128)(2,1)} %copy.67), calls=%async_computation.1 | async-start | bytes 8388608 | tf_op jit(solution)/shard_map/all_to_all | solution.py:162
  577.0 3.9 copy-start.3
  584.6 2.2 copy-start.5
  586.8 2.2 copy-start.4
where the time goes:
time: 643 us; the launch traced here: 635 us
  waiting for transfers between devices  233 us (36%)
  matrix products  174 us (27%)
  local copies, waits for them, and re-layouts  158 us (25%)
  other arithmetic  46.4 us (7%)
  starting transfers between devices  14.5 us (2%)
  between operations  8.86 us (1%)
    all_to_all x1, waiting for transfers between devices, local(): lax.all_to_all(partial_value[None], 'az', split_axis=3, concat_axis=0, ti...  94.4 us
    all_to_all x1, waiting for transfers between devices, local(): lax.all_to_all(folded, 'az', split_axis=0, concat_axis=3, tiled=True)  94 us
    ppermute x2, waiting for transfers between devices, passed_along(): lax.ppermute(value, axis, [(source, source + steps) for source in range(i...  44.5 us
    dot_general x4, matrix products, compress(): jnp.dot(block_table, window, precision=precise, preferred_element_type=jn...  38.2 us
    dot_general x6, matrix products, complex_contract(): jnp.einsum(pattern, real_in, sin_table, precision=precise)  35.9 us
    dot_general x6, matrix products, complex_contract(): jnp.einsum(pattern, imag_in, sin_table, precision=precise)  34.3 us
    dot_general x6, matrix products, complex_contract(): jnp.einsum(pattern, real_in, cos_table, precision=precise)  33.9 us
    dot_general x6, matrix products, complex_contract(): jnp.einsum(pattern, imag_in, cos_table, precision=precise)  32.2 us
  transfers between devices with their start and end apart: 4, of which 3 were waited for; matrix products, arithmetic and copies ran while one was open for 4% of the time, Pallas kernels for 0%

commit v1 on v0

v1 whole, which is shorter than its diff:
```python
import functools
import math

import jax
import jax.numpy as jnp
import ml_dtypes
import numpy as np
from jax import lax
from jax.experimental import pallas as pl
from jax.experimental.pallas import tpu as pltpu
from jax.sharding import PartitionSpec as P

RIM_ROWS = 64
TILE = 128
HALF = 64
CALL_ROWS = 128
VMEM_LIMIT = 56 * 1024 * 1024
bf16 = jnp.bfloat16
f32 = jnp.float32


def passed_along(value, axis, steps):
    count = lax.axis_size(axis)
    initial, last = (max(0, -steps), min(count, count - steps))
    return lax.ppermute(value, axis, [(source, source + steps) for source in range(initial, last)])


def butterfly(values, sign, turn):
    count = len(values)
    if count == 1:
        return values
    even = butterfly(values[0::2], sign, turn)
    odd = butterfly(values[1::2], sign, turn)
    lower, upper = [], []
    for k in range(count // 2):
        if k == 0:
            turned = odd[k]
        elif 4 * k == count:
            turned = turn(odd[k], 0.0, float(sign))
        else:
            angle = sign * 2.0 * math.pi * k / count
            turned = turn(odd[k], math.cos(angle), math.sin(angle))
        lower.append(jax.tree.map(lambda x, y: x + y, even[k], turned))
        upper.append(jax.tree.map(lambda x, y: x - y, even[k], turned))
    return lower + upper


def turn_pair(value, c, s):
    re, im = value
    if c == 0.0:
        return (-im, re) if s > 0 else (im, -re)
    return (re * c - im * s, im * c + re * s)


def split(value):
    high = value.astype(bf16)
    return high, (value - high.astype(f32)).astype(bf16)


def forward_kernel(tiles, blocks, first, second, banks, *refs):
    code_ref = refs[0]
    block_refs = refs[1 : 1 + blocks]
    twist_ref, high_ref, low_ref, out_ref, band, window, comp, spread_high, spread_low = refs[1 + blocks :]
    step = pl.program_id(0)
    rows = tiles * TILE
    span = code_ref.shape[2]

    @pl.when(step == 0)
    def _():
        def shifted(index):
            wide = jnp.broadcast_to(code_ref[index], (TILE, span))
            return split(pltpu.roll(wide, 0, 1, stride=1, stride_axis=0))

        for part, (c, s) in enumerate(zip(shifted(0), shifted(1))):
            at = 2 * TILE * part
            band[at : at + TILE, :span] = c
            band[at : at + TILE, span:] = s
            band[at + TILE : at + 2 * TILE, :span] = -s
            band[at + TILE : at + 2 * TILE, span:] = c

    for index, block_ref in enumerate(block_refs):
        window[:, index * TILE : (index + 1) * TILE, :] = block_ref[...].astype(bf16)
    for tile in range(tiles):
        at = tile * TILE
        both = jnp.concatenate([window[0, at : at + span], window[1, at : at + span]], axis=0)
        product = jnp.dot(band[...], both, preferred_element_type=f32)
        comp[step, 0, at : at + TILE] = product[:TILE] + product[2 * TILE : 3 * TILE]
        comp[step, 1, at : at + TILE] = product[TILE : 2 * TILE] + product[3 * TILE :]

    @pl.when(step == first - 1)
    def _():
        @pl.loop(0, rows // 16)
        def _(chunk):
            at = pl.multiple_of(chunk * 16, 16)
            for lane in range(0, second, 128):
                lanes = slice(lane, lane + 128)
                values = [(comp[a, 0, pl.ds(at, 16), lanes], comp[a, 1, pl.ds(at, 16), lanes]) for a in range(first)]
                values = butterfly(values, -1, turn_pair)
                for k, (re, im) in enumerate(values):
                    c, s = twist_ref[0, k : k + 1, lanes], twist_ref[1, k : k + 1, lanes]
                    where = pl.ds(pl.multiple_of(k * rows + at, 16), 16)
                    for base, value in ((0, re * c + im * s), (second, im * c - re * s)):
                        high, low = split(value)
                        spread_high[where, base + lane : base + lane + 128] = high
                        spread_low[where, base + lane : base + lane + 128] = low

        high = spread_high[...]
        result = (
            jnp.dot(high, high_ref[...], preferred_element_type=f32)
            + jnp.dot(high, low_ref[...], preferred_element_type=f32)
            + jnp.dot(spread_low[...], high_ref[...], preferred_element_type=f32)
        )
        for k in range(first):
            for g in range(banks):
                out_ref[g, :, k * 128 : (k + 1) * 128] = result[
                    k * rows : (k + 1) * rows, g * 128 : (g + 1) * 128
                ].astype(bf16)


def forward_call(code, echo, rims, start, rows, twist, high, low, banks):
    first, second = twist.shape[1:]
    span = code.shape[2]
    tiles = rows // TILE
    blocks = tiles + span // TILE - 1
    own = echo.shape[1] // TILE
    operands, specs = [], []
    for index in range(blocks):
        place = start // TILE + index
        if place < own:
            operands.append(echo)
            specs.append(pl.BlockSpec((2, TILE, second), functools.partial(lambda p, s: (0, p, s), place)))
        else:
            operands.append(rims[place - own])
            specs.append(pl.BlockSpec((2, TILE, second), lambda s: (0, 0, s)))
    whole = lambda shape: pl.BlockSpec(shape, lambda s: (0,) * len(shape))
    return pl.pallas_call(
        functools.partial(forward_kernel, tiles, blocks, first, second, banks),
        grid=(first,),
        in_specs=[whole(code.shape)] + specs + [whole(twist.shape), whole(high.shape), whole(low.shape)],
        out_specs=whole((banks, rows, first * 128)),
        out_shape=jax.ShapeDtypeStruct((banks, rows, first * 128), bf16),
        scratch_shapes=[
            pltpu.VMEM((4 * TILE, 2 * span), bf16),
            pltpu.VMEM((2, blocks * TILE, second), bf16),
            pltpu.VMEM((first, 2, rows, second), f32),
            pltpu.VMEM((first * rows, 2 * second), bf16),
            pltpu.VMEM((first * rows, 2 * second), bf16),
        ],
        compiler_params=pltpu.CompilerParams(vmem_limit_bytes=VMEM_LIMIT),
        cost_estimate=pl.CostEstimate(flops=rows * 24_000_000, bytes_accessed=rows * 30_000, transcendentals=0),
        name="forward",
    )(code, *operands, twist, high, low)


SINE = [(-1) ** n * (2.0 * math.pi) ** (2 * n + 1) / math.factorial(2 * n + 1) for n in range(6)]


def cosine_turns(turns):
    rest = turns - jnp.round(turns)
    u = 0.25 - jnp.abs(rest)
    z = u * u
    total = jnp.full_like(z, SINE[-1])
    for factor in reversed(SINE[:-1]):
        total = total * z + factor
    return total * u


def migrate_kernel(tiles, banks, taps, width, offset_ref, weight_ref, rate_ref, base_ref, own_ref, next_ref, out_ref, band, spec_high, spec_low, moved):
    rows = tiles * TILE
    span = TILE + RIM_ROWS

    @pl.when(pl.program_id(0) == 0)
    def _():
        for b in range(banks):
            steps = lax.broadcasted_iota(jnp.int32, (TILE, span), 1) - lax.broadcasted_iota(jnp.int32, (TILE, span), 0) - offset_ref[b]
            for tile in range(tiles):
                total = jnp.zeros((TILE, span), f32)
                for t in range(taps):
                    total = jnp.where(steps == t, weight_ref[b, tile * TILE : (tile + 1) * TILE, t : t + 1], total)
                high, low = split(total)
                band[b, tile, :TILE] = high
                band[b, tile, TILE:] = low

    lane_id = lax.broadcasted_iota(jnp.int32, (1, 128), 1)
    left = lane_id < HALF
    minus = jnp.where(left, -1.0, 1.0).astype(f32)

    def turn_lanes(value, c, s):
        crossed = pltpu.roll(value, HALF, 1) * minus
        if c == 0.0:
            return crossed if s > 0 else -crossed
        return value * c + crossed * s

    def combine(ref, at, place):
        for lane in range(0, width, 128):
            lanes = slice(lane, lane + 128)
            values = butterfly([ref[a, pl.ds(at, 32), lanes].astype(f32) for a in range(banks)], -1, turn_lanes)
            for b, value in enumerate(values):
                high, low = split(value)
                spec_high[b, pl.ds(place, 32), lanes] = high
                spec_low[b, pl.ds(place, 32), lanes] = low

    @pl.loop(0, rows // 32)
    def _(chunk):
        at = pl.multiple_of(chunk * 32, 32)
        combine(own_ref, at, at)

    for at in range(0, RIM_ROWS, 32):
        combine(next_ref, at, rows + at)

    for b in range(banks):
        for tile in range(tiles):
            at = tile * TILE
            product = jnp.dot(band[b, tile], spec_high[b, at : at + span], preferred_element_type=f32)
            rest = jnp.dot(band[b, tile, :TILE], spec_low[b, at : at + span], preferred_element_type=f32)
            moved[b, at : at + TILE] = product[:TILE] + product[TILE:] + rest

    quarter = jnp.where(left, 0.0, 0.25).astype(f32)

    @pl.loop(0, rows // 32)
    def _(chunk):
        at = pl.ds(pl.multiple_of(chunk * 32, 32), 32)
        rate = rate_ref[at]
        for lane in range(0, width, 128):
            lanes = slice(lane, lane + 128)
            values = []
            for b in range(banks):
                wave = cosine_turns(rate * base_ref[b : b + 1, lanes] - quarter)
                crossed = pltpu.roll(wave, HALF, 1)
                value = moved[b, at, lanes]
                values.append(
                    value * jnp.where(left, wave, crossed)
                    + pltpu.roll(value, HALF, 1) * jnp.where(left, -crossed, wave)
                )
            for a, value in enumerate(butterfly(values, 1, turn_lanes)):
                out_ref[a, at, lanes] = value.astype(bf16)


def migrate_call(offsets, weights, rate, base, own, following, start):
    banks, rows, lanes = own.shape
    taps = weights.shape[2]
    width = min(256, lanes)
    tiles = rows // TILE
    return pl.pallas_call(
        functools.partial(migrate_kernel, tiles, banks, taps, width),
        grid=(lanes // width,),
        in_specs=[
            pl.BlockSpec(memory_space=pltpu.SMEM),
            pl.BlockSpec((banks, rows, taps), lambda s: (0, start // rows, 0)),
            pl.BlockSpec((rows, 128), lambda s: (start // rows, 0)),
            pl.BlockSpec((banks, width), lambda s: (0, s)),
            pl.BlockSpec((banks, rows, width), lambda s: (0, 0, s)),
            pl.BlockSpec((banks, RIM_ROWS, width), lambda s: (0, 0, s)),
        ],
        out_specs=pl.BlockSpec((banks, rows, width), lambda s: (0, 0, s)),
        out_shape=jax.ShapeDtypeStruct(own.shape, bf16),
        scratch_shapes=[
            pltpu.VMEM((banks, tiles, 2 * TILE, TILE + RIM_ROWS), bf16),
            pltpu.VMEM((banks, rows + RIM_ROWS, width), bf16),
            pltpu.VMEM((banks, rows + RIM_ROWS, width), bf16),
            pltpu.VMEM((banks, rows, width), f32),
        ],
        compiler_params=pltpu.CompilerParams(vmem_limit_bytes=VMEM_LIMIT),
        cost_estimate=pl.CostEstimate(flops=rows * 10_000_000, bytes_accessed=rows * 30_000, transcendentals=0),
        name="migrate",
    )(offsets, weights, rate, base, own, following)


def inverse_kernel(first, second, banks, in_ref, twist_ref, high_ref, low_ref, *refs):
    out_ref, gathered, turned = refs[-3:]
    for k in range(first):
        for g in range(banks):
            gathered[k * TILE : (k + 1) * TILE, g * 128 : (g + 1) * 128] = in_ref[g, :, k * 128 : (k + 1) * 128]
    value = gathered[...]
    across = (((1,), (1,)), ((), ()))
    turned[...] = lax.dot_general(value, high_ref[...], across, preferred_element_type=f32) + lax.dot_general(
        value, low_ref[...], across, preferred_element_type=f32
    )

    @pl.loop(0, TILE // 16)
    def _(chunk):
        at = pl.multiple_of(chunk * 16, 16)
        for lane in range(0, second, 128):
            values = []
            for k in range(first):
                where = pl.ds(pl.multiple_of(k * TILE + at, 16), 16)
                re = turned[where, lane : lane + 128]
                im = turned[where, second + lane : second + lane + 128]
                c = twist_ref[0, k : k + 1, lane : lane + 128]
                s = twist_ref[1, k : k + 1, lane : lane + 128]
                values.append((re * c - im * s, im * c + re * s))
            for a, (re, im) in enumerate(butterfly(values, 1, turn_pair)):
                lanes = slice(a * second + lane, a * second + lane + 128)
                out_ref[0, pl.ds(at, 16), lanes] = re
                out_ref[1, pl.ds(at, 16), lanes] = im


def inverse_call(previous, received, twist, high, low, start, total_rows):
    banks, rows, lanes = received.shape
    first, second = twist.shape[1:]
    whole = lambda shape: pl.BlockSpec(shape, lambda s: (0,) * len(shape))
    specs = [pl.BlockSpec((banks, TILE, lanes), lambda s: (0, s, 0)), whole(twist.shape), whole(high.shape), whole(low.shape)]
    operands = [received, twist, high, low]
    aliases = {}
    if previous is not None:
        specs.append(pl.BlockSpec(memory_space=pl.ANY))
        operands.append(previous)
        aliases = {4: 0}
    return pl.pallas_call(
        functools.partial(inverse_kernel, first, second, banks),
        grid=(rows // TILE,),
        in_specs=specs,
        out_specs=pl.BlockSpec((2, TILE, first * second), lambda s: (0, start // TILE + s, 0)),
        out_shape=jax.ShapeDtypeStruct((2, total_rows, first * second), f32),
        scratch_shapes=[
            pltpu.VMEM((first * TILE, 2 * second), bf16),
            pltpu.VMEM((first * TILE, 2 * second), f32),
        ],
        input_output_aliases=aliases,
        compiler_params=pltpu.CompilerParams(vmem_limit_bytes=VMEM_LIMIT),
        cost_estimate=pl.CostEstimate(flops=rows * 10_000_000, bytes_accessed=rows * 30_000, transcendentals=0),
        name="inverse",
    )(*operands)


def tables(banks, first, second):
    pulses = banks * first * second
    inner = np.arange(second)
    highs, lows, twists = [], [], []
    for bank in range(banks):
        steps = banks * inner + bank
        angle = 2.0 * np.pi * ((steps[:, None] * inner[None, :]) % (banks * second)) / (banks * second)
        c, s = np.cos(angle), np.sin(angle)
        re_out = np.concatenate([c, s], axis=0).reshape(2 * second, banks, HALF)
        im_out = np.concatenate([-s, c], axis=0).reshape(2 * second, banks, HALF)
        table = np.stack([re_out, im_out], axis=2).reshape(2 * second, 2 * second)
        high = table.astype(ml_dtypes.bfloat16)
        highs.append(high)
        lows.append((table - high.astype(np.float64)).astype(ml_dtypes.bfloat16))
        angle = 2.0 * np.pi * ((np.arange(first)[:, None] * steps[None, :]) % pulses) / pulses
        twists.append(np.stack([np.cos(angle), np.sin(angle)]).astype(np.float32))
    return np.stack(highs), np.stack(lows), np.stack(twists)


def local(echo_planes, pulse_phase, band_offsets, band_weights, azimuth_rate):
    banks = lax.axis_size("az")
    bank = lax.axis_index("az")
    row_count, pulse_local = echo_planes.shape[1:]
    pulse_count = pulse_local * banks
    second = HALF * banks
    first = pulse_local // second
    code_length = pulse_phase.shape[0]
    reach = -(-code_length // TILE)
    rims = [
        passed_along(echo_planes[:, i * TILE : (i + 1) * TILE].astype(bf16), "rg", -1) for i in range(reach)
    ]
    highs, lows, twists = tables(banks, first, second)
    pick = lambda stack: lax.dynamic_index_in_dim(jnp.asarray(stack), bank, 0, keepdims=False)
    high, low, twist = pick(highs), pick(lows), pick(twists)
    span = (reach + 1) * TILE
    norm_scale = 1.0 / math.sqrt(code_length)
    code = jnp.stack([jnp.cos(pulse_phase), jnp.sin(pulse_phase)]) * norm_scale
    code = jnp.pad(code, ((0, 0), (0, span - code_length)))[:, None, :]

    offsets = band_offsets[:, 0, 0]
    weights = band_weights[:, 0].transpose(0, 2, 1)
    rate = jnp.broadcast_to(azimuth_rate[:, None], (row_count, 128))
    lane = jnp.arange(first * 128, dtype=jnp.int32)
    bins = bank * (HALF * first) + first * (lane % HALF) + lane // 128
    bins = bins[None, :] + pulse_local * jnp.arange(banks, dtype=jnp.int32)[:, None]
    centered = jnp.where(bins < pulse_count // 2, bins, bins - pulse_count)
    frequency = centered.astype(f32) / pulse_count
    base = 0.5 * frequency * frequency

    starts = list(range(0, row_count, CALL_ROWS))
    swap = lambda value: lax.all_to_all(value, "az", split_axis=0, concat_axis=0, tiled=True)
    spectra = [swap(forward_call(code, echo_planes, rims, s, CALL_ROWS, twist, high, low, banks)) for s in starts]
    spectra.append(passed_along(spectra[0][:, :RIM_ROWS], "rg", -1))
    folded = [
        swap(migrate_call(offsets, weights, rate, base, spectra[i], spectra[i + 1], s)) for i, s in enumerate(starts)
    ]
    twist = twist * (1.0 / pulse_count)
    out = None
    for s, value in zip(starts, folded):
        out = inverse_call(out, value, twist, high, low, s, row_count)
    return out


def solution(mesh):
    in_specs = (P(None, "rg", "az"), P(), P(None, "az", "rg"), P(None, "az", None, "rg"), P("rg"))
    out_specs = P(None, "rg", "az")
    return jax.shard_map(local, mesh=mesh, in_specs=in_specs, out_specs=out_specs, check_vma=False)
```

time: 643 us -> 277 us (0.43)
  the two profiles are of different devices: /device:TPU:4 before, /device:TPU:2 now
where the time goes in v1:
time: 277 us; the launch traced here: 276 us
  waiting for transfers between devices  108 us (39%)
  Pallas kernels  101 us (36%)
  starting transfers between devices  45.2 us (16%)
  local copies, waits for them, and re-layouts  15.3 us (6%)
  other arithmetic  6.04 us (2%)
    all_to_all x8, waiting for transfers between devices, local(): lax.all_to_all(value, 'az', split_axis=0, concat_axis=0, tiled=True)  64.1 us
    pallas_call x4, Pallas kernels, forward_call(): pl.pallas_call(functools.partial(forward_kernel, tiles, blocks, first, se...  45.6 us
    ppermute x4, waiting for transfers between devices, passed_along(): lax.ppermute(value, axis, [(source, source + steps) for source in range(i...  43.9 us
    pallas_call x4, Pallas kernels, migrate_call(): pl.pallas_call(functools.partial(migrate_kernel, tiles, banks, taps, widt...  36.7 us
    all_to_all x8, starting transfers between devices, local(): lax.all_to_all(value, 'az', split_axis=0, concat_axis=0, tiled=True)  33.9 us
    pallas_call x4, Pallas kernels, inverse_call(): pl.pallas_call(functools.partial(inverse_kernel, first, second, banks), g...  18.8 us
    ppermute x4, starting transfers between devices, passed_along(): lax.ppermute(value, axis, [(source, source + steps) for source in range(i...  11.3 us
    unnamed x29, local copies, waits for them, and re-layouts  7.03 us
  transfers between devices with their start and end apart: 12, of which 9 were waited for; matrix products, arithmetic and copies ran while one was open for 4% of the time, Pallas kernels for 31%

profile of v1, /device:TPU:2, one launch (start us, length us, event | category | flops | bytes accessed | tf_op | source)
XLA Modules:
  0.0 275.8 jit_solution(13012930117827562721)
XLA Ops:
  5.0 11.7 %forward.5 = bf16[4,128,1024]{2,1,0:T(8,128)(2,1)} custom-call(f32[2,1,512]{2,1,0:T(1,128)} %broadcast_in_dim.5.refs_0_, f32[2,512,2048]{2,1,0:T(8,128)} %refs_3_.3, f32[2,512,2048]{2,1,0:T(8,128)} %refs_3_.3, f32[2,512,2048]{2,1,0:T(8,128)} %refs_3_.3, f32[2,512,2048]{2,1,0:T(8,128)} %refs_3_.3, f32[2,8,256]{2,1,0:T(8,128)} %dynamic-slice_bitcast_fusion.2.refs_5_, ...), custom_call_target="tpu_custom_call" | custom-call | flops 3072000000 | bytes 3840000 | tf_op jit(solution)/shard_map/forward/pallas_call | solution.py:136
  16.7 4.9 %all-to-all-start.1 = ((bf16[4,128,1024]{2,1,0:T(8,128)(2,1)}), bf16[4,128,1024]{2,1,0:T(8,128)(2,1)S(1)}, u32[]{:S(2)}, u32[]{:S(2)}) async-start(bf16[4,128,1024]{2,1,0:T(8,128)(2,1)} %forward.5), calls=%async_computation.1 | async-start | bytes 2097152 | tf_op jit(solution)/shard_map/all_to_all | solution.py:376
  21.6 4.0 %convert.5 = bf16[2,512,2048]{2,1,0:T(8,128)(2,1)S(1)} convert(f32[2,512,2048]{2,1,0:T(8,128)} %refs_3_.3) | non-fusion elementwise | flops 2097152 | bytes 12582912 | tf_op jit(solution)/shard_map/convert.2
  28.9 12.3 %collective-permute-done.refs_2_.refs_3_.refs_4_ = bf16[2,128,2048]{2,1,0:T(8,128)(2,1)S(1)} collective-permute-done((bf16[2,128,2048]{2,1,0:T(8,128)(2,1)S(1)}, bf16[2,128,2048]{2,1,0:T(8,128)(2,1)S(1)}, u32[]{:S(2)}, u32[]{:S(2)}) %collective-permute-start) | collective-permute-done | bytes 1048608 | tf_op jit(solution)/shard_map/ppermute | solution.py:25
  42.1 11.4 %forward.7 = bf16[4,128,1024]{2,1,0:T(8,128)(2,1)} custom-call(f32[2,1,512]{2,1,0:T(1,128)} %broadcast_in_dim.5.refs_0_, f32[2,512,2048]{2,1,0:T(8,128)} %refs_3_.3, f32[2,512,2048]{2,1,0:T(8,128)} %refs_3_.3, f32[2,512,2048]{2,1,0:T(8,128)} %refs_3_.3, bf16[2,128,2048]{2,1,0:T(8,128)(2,1)} %copy-done, f32[2,8,256]{2,1,0:T(8,128)} %dynamic-slice_bitcast_fusion.2.refs_5_, ...), custom_call_target="tpu_custom_call" | custom-call | flops 3072000000 | bytes 3840000 | tf_op jit(solution)/shard_map/forward/pallas_call | solution.py:136
  53.6 5.1 %all-to-all-start.5 = ((bf16[4,128,1024]{2,1,0:T(8,128)(2,1)}), bf16[4,128,1024]{2,1,0:T(8,128)(2,1)S(1)}, u32[]{:S(2)}, u32[]{:S(2)}) async-start(bf16[4,128,1024]{2,1,0:T(8,128)(2,1)} %forward.7), calls=%async_computation.5 | async-start | bytes 2097152 | tf_op jit(solution)/shard_map/all_to_all | solution.py:376
  58.7 3.8 %collective-permute-start.1 = (bf16[2,128,2048]{2,1,0:T(8,128)(2,1)S(1)}, bf16[2,128,2048]{2,1,0:T(8,128)(2,1)S(1)}, u32[]{:S(2)}, u32[]{:S(2)}) collective-permute-start(bf16[2,128,2048]{2,1,0:T(8,128)(2,1)S(1)} %get-tuple-element.6), channel_id=1, source_target_pairs={{1,0},{2,1},{3,2},{4,3},{5,4},{6,5},{7,6},{9,8},{10,9},{11,10},{12... | collective-permute-start | bytes 3145736 | tf_op jit(solution)/shard_map/ppermute | solution.py:25
  62.5 12.3 %collective-permute-done.1.refs_3_.refs_4_ = bf16[2,128,2048]{2,1,0:T(8,128)(2,1)S(1)} collective-permute-done((bf16[2,128,2048]{2,1,0:T(8,128)(2,1)S(1)}, bf16[2,128,2048]{2,1,0:T(8,128)(2,1)S(1)}, u32[]{:S(2)}, u32[]{:S(2)}) %collective-permute-start.1) | collective-permute-done | bytes 1048608 | tf_op jit(solution)/shard_map/ppermute | solution.py:25
  75.8 11.3 %forward.6 = bf16[4,128,1024]{2,1,0:T(8,128)(2,1)} custom-call(f32[2,1,512]{2,1,0:T(1,128)} %broadcast_in_dim.5.refs_0_, f32[2,512,2048]{2,1,0:T(8,128)} %refs_3_.3, f32[2,512,2048]{2,1,0:T(8,128)} %refs_3_.3, bf16[2,128,2048]{2,1,0:T(8,128)(2,1)} %copy-done, bf16[2,128,2048]{2,1,0:T(8,128)(2,1)} %copy-done.1, ...), custom_call_target="tpu_custom_call" | custom-call | flops 3072000000 | bytes 3840000 | tf_op jit(solution)/shard_map/forward/pallas_call | solution.py:136
  87.1 4.8 %all-to-all-start.3 = ((bf16[4,128,1024]{2,1,0:T(8,128)(2,1)}), bf16[4,128,1024]{2,1,0:T(8,128)(2,1)S(1)}, u32[]{:S(2)}, u32[]{:S(2)}) async-start(bf16[4,128,1024]{2,1,0:T(8,128)(2,1)} %forward.6), calls=%async_computation.3 | async-start | bytes 2097152 | tf_op jit(solution)/shard_map/all_to_all | solution.py:376
  91.9 3.7 %collective-permute-start.2 = (bf16[2,128,2048]{2,1,0:T(8,128)(2,1)}, bf16[2,128,2048]{2,1,0:T(8,128)(2,1)S(1)}, u32[]{:S(2)}, u32[]{:S(2)}) collective-permute-start(bf16[2,128,2048]{2,1,0:T(8,128)(2,1)} %get-tuple-element.5), channel_id=1, source_target_pairs={{1,0},{2,1},{3,2},{4,3},{5,4},{6,5},{7,6},{9,8},{10,9},{11,10},{12... | collective-permute-start | bytes 3145736 | tf_op jit(solution)/shard_map/ppermute | solution.py:25
  95.6 12.6 %collective-permute-done.2.refs_4_ = bf16[2,128,2048]{2,1,0:T(8,128)(2,1)S(1)} collective-permute-done((bf16[2,128,2048]{2,1,0:T(8,128)(2,1)}, bf16[2,128,2048]{2,1,0:T(8,128)(2,1)S(1)}, u32[]{:S(2)}, u32[]{:S(2)}) %collective-permute-start.2) | collective-permute-done | bytes 1048608 | tf_op jit(solution)/shard_map/ppermute | solution.py:25
  109.2 11.2 %forward.4 = bf16[4,128,1024]{2,1,0:T(8,128)(2,1)} custom-call(f32[2,1,512]{2,1,0:T(1,128)} %broadcast_in_dim.5.refs_0_, f32[2,512,2048]{2,1,0:T(8,128)} %refs_3_.3, bf16[2,128,2048]{2,1,0:T(8,128)(2,1)} %copy-done, bf16[2,128,2048]{2,1,0:T(8,128)(2,1)} %copy-done.1, bf16[2,128,2048]{2,1,0:T(8,128)(2,1)} %copy-done.7, ...), custom_call_target="tpu_custom_call" | custom-call | flops 3072000000 | bytes 3840000 | tf_op jit(solution)/shard_map/forward/pallas_call | solution.py:136
  120.4 4.8 %all-to-all-start = ((bf16[4,128,1024]{2,1,0:T(8,128)(2,1)}), bf16[4,128,1024]{2,1,0:T(8,128)(2,1)S(1)}, u32[]{:S(2)}, u32[]{:S(2)}) async-start(bf16[4,128,1024]{2,1,0:T(8,128)(2,1)} %forward.4), calls=%async_computation | async-start | bytes 2097152 | tf_op jit(solution)/shard_map/all_to_all | solution.py:376
  128.1 9.1 %migrate.7 = bf16[4,128,1024]{2,1,0:T(8,128)(2,1)} custom-call(s32[4]{0:T(128)} %bitcast.16, f32[4,512,8]{2,1,0:T(8,128)} %bitcast.12, f32[512,128]{1,0:T(8,128)} %broadcast_in_dim.4.rate_ref, f32[4,1024]{1,0:T(4,128)} %multiply_multiply_fusion.base_ref, bf16[4,128,1024]{2,1,0:T(8,128)(2,1)} %copy-done.6, bf16[4,128,1024]{2,1,0:T(8,128)(2,1)} %copy-done.8), custom_call_target="tpu_custom_call" | custom-call | flops 1280000000 | bytes 3840000 | tf_op jit(solution)/shard_map/migrate/pallas_call | solution.py:244
  137.2 14.1 %all-to-all-done.own_ref.next_ref = bf16[4,128,1024]{2,1,0:T(8,128)(2,1)S(1)} async-done(((bf16[4,128,1024]{2,1,0:T(8,128)(2,1)}), bf16[4,128,1024]{2,1,0:T(8,128)(2,1)S(1)}, u32[]{:S(2)}, u32[]{:S(2)}) %all-to-all-start) | async-done | bytes 1048608 | tf_op jit(solution)/shard_map/all_to_all | solution.py:376
  152.3 3.5 %all-to-all-start.7 = ((bf16[4,128,1024]{2,1,0:T(8,128)(2,1)}), bf16[4,128,1024]{2,1,0:T(8,128)(2,1)S(1)}, u32[]{:S(2)}, u32[]{:S(2)}) async-start(bf16[4,128,1024]{2,1,0:T(8,128)(2,1)} %migrate.7), calls=%async_computation.7 | async-start | bytes 2097152 | tf_op jit(solution)/shard_map/all_to_all | solution.py:376
  155.8 9.2 %migrate.6 = bf16[4,128,1024]{2,1,0:T(8,128)(2,1)} custom-call(s32[4]{0:T(128)} %bitcast.17, f32[4,512,8]{2,1,0:T(8,128)} %bitcast.13, f32[512,128]{1,0:T(8,128)} %broadcast_in_dim.4.rate_ref, f32[4,1024]{1,0:T(4,128)} %multiply_multiply_fusion.base_ref, bf16[4,128,1024]{2,1,0:T(8,128)(2,1)} %copy-done.8, bf16[4,128,1024]{2,1,0:T(8,128)(2,1)} %copy-done.9), custom_call_target="tpu_custom_call" | custom-call | flops 1280000000 | bytes 3840000 | tf_op jit(solution)/shard_map/migrate/pallas_call | solution.py:244
  165.0 17.8 %all-to-all-done.7.in_ref = bf16[4,128,1024]{2,1,0:T(8,128)(2,1)S(1)} async-done(((bf16[4,128,1024]{2,1,0:T(8,128)(2,1)}), bf16[4,128,1024]{2,1,0:T(8,128)(2,1)S(1)}, u32[]{:S(2)}, u32[]{:S(2)}) %all-to-all-start.7) | async-done | bytes 1048608 | tf_op jit(solution)/shard_map/all_to_all | solution.py:376
  182.8 3.7 %all-to-all-start.6 = ((bf16[4,128,1024]{2,1,0:T(8,128)(2,1)}), bf16[4,128,1024]{2,1,0:T(8,128)(2,1)S(1)}, u32[]{:S(2)}, u32[]{:S(2)}) async-start(bf16[4,128,1024]{2,1,0:T(8,128)(2,1)} %migrate.6), calls=%async_computation.6 | async-start | bytes 2097152 | tf_op jit(solution)/shard_map/all_to_all | solution.py:376
  186.5 9.2 %migrate.5 = bf16[4,128,1024]{2,1,0:T(8,128)(2,1)} custom-call(s32[4]{0:T(128)} %bitcast.18, f32[4,512,8]{2,1,0:T(8,128)} %bitcast.14, f32[512,128]{1,0:T(8,128)} %broadcast_in_dim.4.rate_ref, f32[4,1024]{1,0:T(4,128)} %multiply_multiply_fusion.base_ref, bf16[4,128,1024]{2,1,0:T(8,128)(2,1)} %copy-done.9, bf16[4,128,1024]{2,1,0:T(8,128)(2,1)} %copy-done.10), custom_call_target="tpu_custom_call" | custom-call | flops 1280000000 | bytes 3840000 | tf_op jit(solution)/shard_map/migrate/pallas_call | solution.py:244
  195.7 16.8 %all-to-all-done.6.in_ref = bf16[4,128,1024]{2,1,0:T(8,128)(2,1)S(1)} async-done(((bf16[4,128,1024]{2,1,0:T(8,128)(2,1)}), bf16[4,128,1024]{2,1,0:T(8,128)(2,1)S(1)}, u32[]{:S(2)}, u32[]{:S(2)}) %all-to-all-start.6) | async-done | bytes 1048608 | tf_op jit(solution)/shard_map/all_to_all | solution.py:376
  212.5 3.5 %all-to-all-start.4 = ((bf16[4,128,1024]{2,1,0:T(8,128)(2,1)}), bf16[4,128,1024]{2,1,0:T(8,128)(2,1)S(1)}, u32[]{:S(2)}, u32[]{:S(2)}) async-start(bf16[4,128,1024]{2,1,0:T(8,128)(2,1)} %migrate.5), calls=%async_computation.4 | async-start | bytes 2097152 | tf_op jit(solution)/shard_map/all_to_all | solution.py:376
  219.1 6.7 %collective-permute-done.3.next_ref = bf16[4,64,1024]{2,1,0:T(8,128)(2,1)S(1)} collective-permute-done((bf16[4,64,1024]{2,1,0:T(8,128)(2,1)S(1)}, bf16[4,64,1024]{2,1,0:T(8,128)(2,1)S(1)}, u32[]{:S(2)}, u32[]{:S(2)}) %collective-permute-start.3) | collective-permute-done | bytes 524320 | tf_op jit(solution)/shard_map/ppermute | solution.py:25
  226.5 9.1 %migrate.4 = bf16[4,128,1024]{2,1,0:T(8,128)(2,1)} custom-call(s32[4]{0:T(128)} %bitcast.19, f32[4,512,8]{2,1,0:T(8,128)} %bitcast.15, f32[512,128]{1,0:T(8,128)} %broadcast_in_dim.4.rate_ref, f32[4,1024]{1,0:T(4,128)} %multiply_multiply_fusion.base_ref, bf16[4,128,1024]{2,1,0:T(8,128)(2,1)} %copy-done.10, bf16[4,64,1024]{2,1,0:T(8,128)(2,1)} %copy-done.13), custom_call_target="tpu_custom_call" | custom-call | flops 1280000000 | bytes 3840000 | tf_op jit(solution)/shard_map/migrate/pallas_call | solution.py:244
  235.7 5.7 %all-to-all-done.4.in_ref = bf16[4,128,1024]{2,1,0:T(8,128)(2,1)S(1)} async-done(((bf16[4,128,1024]{2,1,0:T(8,128)(2,1)}), bf16[4,128,1024]{2,1,0:T(8,128)(2,1)S(1)}, u32[]{:S(2)}, u32[]{:S(2)}) %all-to-all-start.4) | async-done | bytes 1048608 | tf_op jit(solution)/shard_map/all_to_all | solution.py:376
  241.4 3.5 %all-to-all-start.2 = ((bf16[4,128,1024]{2,1,0:T(8,128)(2,1)}), bf16[4,128,1024]{2,1,0:T(8,128)(2,1)S(1)}, u32[]{:S(2)}, u32[]{:S(2)}) async-start(bf16[4,128,1024]{2,1,0:T(8,128)(2,1)} %migrate.4), calls=%async_computation.2 | async-start | bytes 2097152 | tf_op jit(solution)/shard_map/all_to_all | solution.py:376
  246.2 4.7 %inverse.4.refs_0_ = f32[2,512,2048]{2,1,0:T(8,128)} custom-call(bf16[4,128,1024]{2,1,0:T(8,128)(2,1)} %copy-done.2, f32[2,8,256]{2,1,0:T(8,128)} %broadcast_multiply_fusion.twist_ref, bf16[512,512]{1,0:T(8,128)(2,1)} %get-tuple-element.11.refs_6_.high_ref, bf16[512,512]{1,0:T(8,128)(2,1)} %get-tuple-element.10.refs_7_.low_ref), custom_call_target="tpu_custom_call" | custom-call | flops 1280000000 | bytes 3840000 | tf_op jit(solution)/shard_map/inverse/pallas_call | solution.py:309
  250.9 4.7 %inverse.5.refs_0_ = f32[2,512,2048]{2,1,0:T(8,128)} custom-call(bf16[4,128,1024]{2,1,0:T(8,128)(2,1)} %copy-done.3, f32[2,8,256]{2,1,0:T(8,128)} %broadcast_multiply_fusion.twist_ref, bf16[512,512]{1,0:T(8,128)(2,1)} %get-tuple-element.11.refs_6_.high_ref, bf16[512,512]{1,0:T(8,128)(2,1)} %get-tuple-element.10.refs_7_.low_ref, ...), custom_call_target="tpu_custom_call", output_to_operand_aliasing={{}: (4, {})} | custom-call | flops 1280000000 | bytes 3840000 | tf_op jit(solution)/shard_map/inverse/pallas_call | solution.py:309
  255.6 4.7 %inverse.6.refs_0_ = f32[2,512,2048]{2,1,0:T(8,128)} custom-call(bf16[4,128,1024]{2,1,0:T(8,128)(2,1)} %copy-done.4, f32[2,8,256]{2,1,0:T(8,128)} %broadcast_multiply_fusion.twist_ref, bf16[512,512]{1,0:T(8,128)(2,1)} %get-tuple-element.11.refs_6_.high_ref, bf16[512,512]{1,0:T(8,128)(2,1)} %get-tuple-element.10.refs_7_.low_ref, ...), custom_call_target="tpu_custom_call", output_to_operand_aliasing={{}: (4, {})} | custom-call | flops 1280000000 | bytes 3840000 | tf_op jit(solution)/shard_map/inverse/pallas_call | solution.py:309
  260.3 9.7 %all-to-all-done.2.in_ref = bf16[4,128,1024]{2,1,0:T(8,128)(2,1)S(1)} async-done(((bf16[4,128,1024]{2,1,0:T(8,128)(2,1)}), bf16[4,128,1024]{2,1,0:T(8,128)(2,1)S(1)}, u32[]{:S(2)}, u32[]{:S(2)}) %all-to-all-start.2) | async-done | bytes 1048608 | tf_op jit(solution)/shard_map/all_to_all | solution.py:376
  271.1 4.7 %inverse.7 = f32[2,512,2048]{2,1,0:T(8,128)} custom-call(bf16[4,128,1024]{2,1,0:T(8,128)(2,1)} %copy-done.5, f32[2,8,256]{2,1,0:T(8,128)} %broadcast_multiply_fusion.twist_ref, bf16[512,512]{1,0:T(8,128)(2,1)} %get-tuple-element.11.refs_6_.high_ref, bf16[512,512]{1,0:T(8,128)(2,1)} %get-tuple-element.10.refs_7_.low_ref, ...), custom_call_target="tpu_custom_call", output_to_operand_aliasing={{}: (4, {})} | custom-call | flops 1280000000 | bytes 3840000 | tf_op jit(solution)/shard_map/inverse/pallas_call | solution.py:309
  (49 shorter events, 21.1 us)
Async XLA Ops:
  16.7 36.8 %all-to-all-start.1 = ((bf16[4,128,1024]{2,1,0:T(8,128)(2,1)}), bf16[4,128,1024]{2,1,0:T(8,128)(2,1)S(1)}, u32[]{:S(2)}, u32[]{:S(2)}) async-start(bf16[4,128,1024]{2,1,0:T(8,128)(2,1)} %forward.5), calls=%async_computation.1 | async-start | bytes 2097152 | tf_op jit(solution)/shard_map/all_to_all | solution.py:376
  26.9 14.2 %collective-permute-start = (bf16[2,128,2048]{2,1,0:T(8,128)(2,1)S(1)}, bf16[2,128,2048]{2,1,0:T(8,128)(2,1)S(1)}, u32[]{:S(2)}, u32[]{:S(2)}) collective-permute-start(bf16[2,128,2048]{2,1,0:T(8,128)(2,1)S(1)} %get-tuple-element.7), channel_id=1, source_target_pairs={{1,0},{2,1},{3,2},{4,3},{5,4},{6,5},{7,6},{9,8},{10,9},{11,10},{12... | collective-permute-start | bytes 3145736 | tf_op jit(solution)/shard_map/ppermute | solution.py:25
  41.2 1.0 copy-start
  53.6 33.5 %copy-start.6 = (bf16[4,128,1024]{2,1,0:T(8,128)(2,1)}, bf16[4,128,1024]{2,1,0:T(8,128)(2,1)S(1)}, u32[]{:S(2)}) copy-start(bf16[4,128,1024]{2,1,0:T(8,128)(2,1)S(1)} %all-to-all-done.1.own_ref) | copy-start | bytes 3145732
  53.6 33.5 %all-to-all-start.5 = ((bf16[4,128,1024]{2,1,0:T(8,128)(2,1)}), bf16[4,128,1024]{2,1,0:T(8,128)(2,1)S(1)}, u32[]{:S(2)}, u32[]{:S(2)}) async-start(bf16[4,128,1024]{2,1,0:T(8,128)(2,1)} %forward.7), calls=%async_computation.5 | async-start | bytes 2097152 | tf_op jit(solution)/shard_map/all_to_all | solution.py:376
  58.7 16.1 %collective-permute-start.1 = (bf16[2,128,2048]{2,1,0:T(8,128)(2,1)S(1)}, bf16[2,128,2048]{2,1,0:T(8,128)(2,1)S(1)}, u32[]{:S(2)}, u32[]{:S(2)}) collective-permute-start(bf16[2,128,2048]{2,1,0:T(8,128)(2,1)S(1)} %get-tuple-element.6), channel_id=1, source_target_pairs={{1,0},{2,1},{3,2},{4,3},{5,4},{6,5},{7,6},{9,8},{10,9},{11,10},{12... | collective-permute-start | bytes 3145736 | tf_op jit(solution)/shard_map/ppermute | solution.py:25
  74.8 1.0 copy-start.1
  87.1 33.3 %copy-start.8 = (bf16[4,128,1024]{2,1,0:T(8,128)(2,1)}, bf16[4,128,1024]{2,1,0:T(8,128)(2,1)S(1)}, u32[]{:S(2)}) copy-start(bf16[4,128,1024]{2,1,0:T(8,128)(2,1)S(1)} %all-to-all-done.5.own_ref.next_ref) | copy-start | bytes 3145732
  87.1 33.3 %all-to-all-start.3 = ((bf16[4,128,1024]{2,1,0:T(8,128)(2,1)}), bf16[4,128,1024]{2,1,0:T(8,128)(2,1)S(1)}, u32[]{:S(2)}, u32[]{:S(2)}) async-start(bf16[4,128,1024]{2,1,0:T(8,128)(2,1)} %forward.6), calls=%async_computation.3 | async-start | bytes 2097152 | tf_op jit(solution)/shard_map/all_to_all | solution.py:376
  91.9 33.3 %copy-start.11 = (f32[4,1,8,512]{3,2,1,0:T(8,128)S(1)}, f32[4,1,8,512]{3,2,1,0:T(8,128)}, u32[]{:S(2)}) copy-start(f32[4,1,8,512]{3,2,1,0:T(8,128)} %param.11) | copy-start | bytes 196612
  91.9 35.3 %copy-start.12 = (f32[512]{0:T(512)S(1)}, f32[512]{0:T(512)}, u32[]{:S(2)}) copy-start(f32[512]{0:T(512)} %param.12) | copy-start | bytes 6148
  91.9 16.3 %collective-permute-start.2 = (bf16[2,128,2048]{2,1,0:T(8,128)(2,1)}, bf16[2,128,2048]{2,1,0:T(8,128)(2,1)S(1)}, u32[]{:S(2)}, u32[]{:S(2)}) collective-permute-start(bf16[2,128,2048]{2,1,0:T(8,128)(2,1)} %get-tuple-element.5), channel_id=1, source_target_pairs={{1,0},{2,1},{3,2},{4,3},{5,4},{6,5},{7,6},{9,8},{10,9},{11,10},{12... | collective-permute-start | bytes 3145736 | tf_op jit(solution)/shard_map/ppermute | solution.py:25
  108.2 1.0 copy-start.7
  120.4 31.9 %copy-start.9 = (bf16[4,128,1024]{2,1,0:T(8,128)(2,1)}, bf16[4,128,1024]{2,1,0:T(8,128)(2,1)S(1)}, u32[]{:S(2)}) copy-start(bf16[4,128,1024]{2,1,0:T(8,128)(2,1)S(1)} %all-to-all-done.3.own_ref.next_ref) | copy-start | bytes 3145732
  120.4 30.9 %all-to-all-start = ((bf16[4,128,1024]{2,1,0:T(8,128)(2,1)}), bf16[4,128,1024]{2,1,0:T(8,128)(2,1)S(1)}, u32[]{:S(2)}, u32[]{:S(2)}) async-start(bf16[4,128,1024]{2,1,0:T(8,128)(2,1)} %forward.4), calls=%async_computation | async-start | bytes 2097152 | tf_op jit(solution)/shard_map/all_to_all | solution.py:376
  151.3 1.0 copy-start.10
  152.3 30.5 %all-to-all-start.7 = ((bf16[4,128,1024]{2,1,0:T(8,128)(2,1)}), bf16[4,128,1024]{2,1,0:T(8,128)(2,1)S(1)}, u32[]{:S(2)}, u32[]{:S(2)}) async-start(bf16[4,128,1024]{2,1,0:T(8,128)(2,1)} %migrate.7), calls=%async_computation.7 | async-start | bytes 2097152 | tf_op jit(solution)/shard_map/all_to_all | solution.py:376
  182.8 29.7 %copy-start.2 = (bf16[4,128,1024]{2,1,0:T(8,128)(2,1)}, bf16[4,128,1024]{2,1,0:T(8,128)(2,1)S(1)}, u32[]{:S(2)}) copy-start(bf16[4,128,1024]{2,1,0:T(8,128)(2,1)S(1)} %all-to-all-done.7.in_ref) | copy-start | bytes 3145732
  182.8 29.7 %all-to-all-start.6 = ((bf16[4,128,1024]{2,1,0:T(8,128)(2,1)}), bf16[4,128,1024]{2,1,0:T(8,128)(2,1)S(1)}, u32[]{:S(2)}, u32[]{:S(2)}) async-start(bf16[4,128,1024]{2,1,0:T(8,128)(2,1)} %migrate.6), calls=%async_computation.6 | async-start | bytes 2097152 | tf_op jit(solution)/shard_map/all_to_all | solution.py:376
  212.5 28.9 %copy-start.3 = (bf16[4,128,1024]{2,1,0:T(8,128)(2,1)}, bf16[4,128,1024]{2,1,0:T(8,128)(2,1)S(1)}, u32[]{:S(2)}) copy-start(bf16[4,128,1024]{2,1,0:T(8,128)(2,1)S(1)} %all-to-all-done.6.in_ref) | copy-start | bytes 3145732
  212.5 28.9 %all-to-all-start.4 = ((bf16[4,128,1024]{2,1,0:T(8,128)(2,1)}), bf16[4,128,1024]{2,1,0:T(8,128)(2,1)S(1)}, u32[]{:S(2)}, u32[]{:S(2)}) async-start(bf16[4,128,1024]{2,1,0:T(8,128)(2,1)} %migrate.5), calls=%async_computation.4 | async-start | bytes 2097152 | tf_op jit(solution)/shard_map/all_to_all | solution.py:376
  217.1 8.6 %collective-permute-start.3 = (bf16[4,64,1024]{2,1,0:T(8,128)(2,1)S(1)}, bf16[4,64,1024]{2,1,0:T(8,128)(2,1)S(1)}, u32[]{:S(2)}, u32[]{:S(2)}) collective-permute-start(bf16[4,64,1024]{2,1,0:T(8,128)(2,1)S(1)} %slice.22), channel_id=1, source_target_pairs={{1,0},{2,1},{3,2},{4,3},{5,4},{6,5},{7,6},{9,8},{10,9},{11,10},{12... | collective-permute-start | bytes 1572872 | tf_op jit(solution)/shard_map/ppermute | solution.py:25
  225.7 0.8 copy-start.13
  241.4 9.6 %copy-start.4 = (bf16[4,128,1024]{2,1,0:T(8,128)(2,1)}, bf16[4,128,1024]{2,1,0:T(8,128)(2,1)S(1)}, u32[]{:S(2)}) copy-start(bf16[4,128,1024]{2,1,0:T(8,128)(2,1)S(1)} %all-to-all-done.4.in_ref) | copy-start | bytes 3145732
  241.4 28.7 %all-to-all-start.2 = ((bf16[4,128,1024]{2,1,0:T(8,128)(2,1)}), bf16[4,128,1024]{2,1,0:T(8,128)(2,1)S(1)}, u32[]{:S(2)}, u32[]{:S(2)}) async-start(bf16[4,128,1024]{2,1,0:T(8,128)(2,1)} %migrate.4), calls=%async_computation.2 | async-start | bytes 2097152 | tf_op jit(solution)/shard_map/all_to_all | solution.py:376
  270.1 1.0 copy-start.5

commit v2 on v1

v2 whole, which is shorter than its diff:
```python
import functools
import math

import jax
import jax.numpy as jnp
import ml_dtypes
import numpy as np
from jax import lax
from jax.experimental import pallas as pl
from jax.experimental.pallas import tpu as pltpu
from jax.sharding import PartitionSpec as P

RIM_ROWS = 64
TILE = 128
HALF = 64
VMEM_LIMIT = 56 * 1024 * 1024
bf16 = jnp.bfloat16
f32 = jnp.float32


def butterfly(values, sign, turn):
    count = len(values)
    if count == 1:
        return values
    even = butterfly(values[0::2], sign, turn)
    odd = butterfly(values[1::2], sign, turn)
    lower, upper = [], []
    for k in range(count // 2):
        if k == 0:
            turned = odd[k]
        elif 4 * k == count:
            turned = turn(odd[k], 0.0, float(sign))
        else:
            angle = sign * 2.0 * math.pi * k / count
            turned = turn(odd[k], math.cos(angle), math.sin(angle))
        lower.append(jax.tree.map(lambda x, y: x + y, even[k], turned))
        upper.append(jax.tree.map(lambda x, y: x - y, even[k], turned))
    return lower + upper


def turn_pair(value, c, s):
    re, im = value
    if c == 0.0:
        return (-im, re) if s > 0 else (im, -re)
    return (re * c - im * s, im * c + re * s)


def split(value):
    high = value.astype(bf16)
    return high, (value - high.astype(f32)).astype(bf16)


SINE = [(-1) ** n * (2.0 * math.pi) ** (2 * n + 1) / math.factorial(2 * n + 1) for n in range(6)]


def cosine_turns(turns):
    rest = turns - jnp.round(turns)
    u = 0.25 - jnp.abs(rest)
    z = u * u
    total = jnp.full_like(z, SINE[-1])
    for factor in reversed(SINE[:-1]):
        total = total * z + factor
    return total * u


def focus_kernel(
    banks, first, second, taps, echo_ref, code_ref, twist_ref, high_ref, low_ref, offset_ref, weight_ref, rate_ref, base_ref, out_ref,
    stage, window, band, comp, spread_high, spread_low, result, send, spectra, taps_band, spec_high, spec_low, moved, folded,
    load_sem, rim_send, rim_recv, out_send, out_recv, edge_send, edge_recv, back_send, back_recv, own_sem,
):
    bank, block = lax.axis_index("az"), lax.axis_index("rg")
    block_count = lax.axis_size("rg")
    rows = echo_ref.shape[1]
    chunks = rows // TILE
    span = code_ref.shape[2]
    reach = span // TILE - 1
    width = min(256, first * 128)
    wide = TILE + RIM_ROWS
    has_next = block < block_count - 1
    has_previous = block > 0

    def load(chunk):
        at = slice(chunk * TILE, (chunk + 1) * TILE)
        return pltpu.make_async_copy(echo_ref.at[:, at], stage.at[:, at], load_sem.at[chunk])

    def rim(piece):
        return pltpu.make_async_remote_copy(
            src_ref=window.at[:, pl.ds(piece * TILE, TILE)],
            dst_ref=window.at[:, pl.ds(rows + piece * TILE, TILE)],
            send_sem=rim_send.at[piece],
            recv_sem=rim_recv.at[piece],
            device_id={"rg": lax.rem(block + block_count - 1, block_count)},
            device_id_type=pl.DeviceIdType.MESH,
        )

    def edge():
        return pltpu.make_async_remote_copy(
            src_ref=spectra.at[:, pl.ds(0, RIM_ROWS)],
            dst_ref=spectra.at[:, pl.ds(rows, RIM_ROWS)],
            send_sem=edge_send,
            recv_sem=edge_recv,
            device_id={"rg": lax.rem(block + block_count - 1, block_count)},
            device_id_type=pl.DeviceIdType.MESH,
        )

    def exchange(source, target, send_sem, recv_sem, chunk, distance):
        peer = lax.rem(bank + distance, banks)
        return pltpu.make_async_remote_copy(
            src_ref=source.at[peer, pl.ds(pl.multiple_of(chunk * TILE, TILE), TILE)],
            dst_ref=target.at[bank, pl.ds(pl.multiple_of(chunk * TILE, TILE), TILE)],
            send_sem=send_sem.at[chunk, distance - 1],
            recv_sem=recv_sem.at[chunk, distance - 1],
            device_id={"az": peer},
            device_id_type=pl.DeviceIdType.MESH,
        )

    outward = functools.partial(exchange, send, spectra, out_send, out_recv)
    backward = functools.partial(exchange, folded, out_ref, back_send, back_recv)

    def own_back(chunk):
        at = pl.ds(pl.multiple_of(chunk * TILE, TILE), TILE)
        return pltpu.make_async_copy(folded.at[bank, at], out_ref.at[bank, at], own_sem.at[chunk])

    for chunk in range(chunks):
        load(chunk).start()

    barrier = pltpu.get_barrier_semaphore()
    for distance in range(1, banks):
        pl.semaphore_signal(
            barrier, inc=1, device_id={"az": lax.rem(bank + distance, banks)}, device_id_type=pl.DeviceIdType.MESH
        )

    @pl.when(has_previous)
    def _():
        pl.semaphore_signal(barrier, inc=1, device_id={"rg": block - 1}, device_id_type=pl.DeviceIdType.MESH)

    @pl.when(has_next)
    def _():
        pl.semaphore_signal(barrier, inc=1, device_id={"rg": block + 1}, device_id_type=pl.DeviceIdType.MESH)

    pl.semaphore_wait(barrier, banks - 1 + has_previous.astype(jnp.int32) + has_next.astype(jnp.int32))

    for chunk in range(chunks):
        load(chunk).wait()

        @pl.loop(0, TILE // 16)
        def _(step):
            at = pl.ds(pl.multiple_of(chunk * TILE + step * 16, 16), 16)
            window[:, at] = stage[:, at].astype(bf16)

        if chunk < reach:

            @pl.when(has_previous)
            def _():
                rim(chunk).start()

    @pl.when(jnp.logical_not(has_next))
    def _():
        window[:, rows : rows + reach * TILE] = jnp.zeros((2, reach * TILE, first * second), bf16)
        spectra[:, rows : rows + RIM_ROWS] = jnp.zeros((banks, RIM_ROWS, first * 128), bf16)

    def shifted(index):
        whole = jnp.broadcast_to(code_ref[index], (TILE, span))
        return split(pltpu.roll(whole, 0, 1, stride=1, stride_axis=0))

    for part, (c, s) in enumerate(zip(shifted(0), shifted(1))):
        at = 2 * TILE * part
        band[at : at + TILE, :span] = c
        band[at : at + TILE, span:] = s
        band[at + TILE : at + 2 * TILE, :span] = -s
        band[at + TILE : at + 2 * TILE, span:] = c

    @pl.loop(0, chunks)
    def _(chunk):
        start = pl.multiple_of(chunk * TILE, TILE)

        @pl.when(jnp.logical_and(has_next, jnp.logical_and(chunk > 0, chunk <= reach)))
        def _():
            rim(chunk - 1).wait_recv()

        @pl.loop(0, first)
        def _(step):
            lanes = pl.ds(pl.multiple_of(step * second, second), second)
            both = jnp.concatenate([window[0, pl.ds(start, span), lanes], window[1, pl.ds(start, span), lanes]], axis=0)
            product = jnp.dot(band[...], both, preferred_element_type=f32)
            comp[step, 0] = product[:TILE] + product[2 * TILE : 3 * TILE]
            comp[step, 1] = product[TILE : 2 * TILE] + product[3 * TILE :]

        @pl.loop(0, TILE // 16)
        def _(step):
            at = pl.multiple_of(step * 16, 16)
            for lane in range(0, second, 128):
                lanes = slice(lane, lane + 128)
                values = [(comp[a, 0, pl.ds(at, 16), lanes], comp[a, 1, pl.ds(at, 16), lanes]) for a in range(first)]
                values = butterfly(values, -1, turn_pair)
                for k, (re, im) in enumerate(values):
                    c, s = twist_ref[0, k : k + 1, lanes], twist_ref[1, k : k + 1, lanes]
                    where = pl.ds(pl.multiple_of(k * TILE + at, 16), 16)
                    for base, value in ((0, re * c + im * s), (second, im * c - re * s)):
                        high, low = split(value)
                        spread_high[where, base + lane : base + lane + 128] = high
                        spread_low[where, base + lane : base + lane + 128] = low

        high = spread_high[...]
        result[...] = (
            jnp.dot(high, high_ref[...], preferred_element_type=f32)
            + jnp.dot(high, low_ref[...], preferred_element_type=f32)
            + jnp.dot(spread_low[...], high_ref[...], preferred_element_type=f32)
        )
        for k in range(first):
            for g in range(banks):
                send[g, pl.ds(start, TILE), k * 128 : (k + 1) * 128] = result[
                    k * TILE : (k + 1) * TILE, g * 128 : (g + 1) * 128
                ].astype(bf16)
        for distance in range(1, banks):
            outward(chunk, distance).start()
        spectra[bank, pl.ds(start, TILE)] = send[bank, pl.ds(start, TILE)]

    for distance in range(1, banks):
        outward(0, distance).wait_recv()

    @pl.when(has_previous)
    def _():
        edge().start()

    left = lax.broadcasted_iota(jnp.int32, (1, 128), 1) < HALF
    minus = jnp.where(left, -1.0, 1.0).astype(f32)
    quarter = jnp.where(left, 0.0, 0.25).astype(f32)

    def turn_lanes(value, c, s):
        crossed = pltpu.roll(value, HALF, 1) * minus
        if c == 0.0:
            return crossed if s > 0 else -crossed
        return value * c + crossed * s

    @pl.loop(0, chunks)
    def _(chunk):
        start = pl.multiple_of(chunk * TILE, TILE)

        @pl.when(chunk < chunks - 1)
        def _():
            for distance in range(1, banks):
                outward(chunk + 1, distance).wait_recv()

        @pl.when(jnp.logical_and(chunk == chunks - 1, has_next))
        def _():
            edge().wait_recv()

        for b in range(banks):
            steps = (
                lax.broadcasted_iota(jnp.int32, (TILE, wide), 1)
                - lax.broadcasted_iota(jnp.int32, (TILE, wide), 0)
                - offset_ref[b]
            )
            total = jnp.zeros((TILE, wide), f32)
            for t in range(taps):
                total = jnp.where(steps == t, weight_ref[b, pl.ds(start, TILE), t : t + 1], total)
            high, low = split(total)
            taps_band[b, :TILE] = high
            taps_band[b, TILE:] = low

        @pl.loop(0, first * 128 // width)
        def _(part):
            offset = pl.multiple_of(part * width, width)

            @pl.loop(0, wide // 32)
            def _(step):
                at = pl.multiple_of(step * 32, 32)
                for lane in range(0, width, 128):
                    lanes = pl.ds(pl.multiple_of(offset + lane, 128), 128)
                    values = [spectra[a, pl.ds(start + at, 32), lanes].astype(f32) for a in range(banks)]
                    for b, value in enumerate(butterfly(values, -1, turn_lanes)):
                        high, low = split(value)
                        spec_high[b, pl.ds(at, 32), lane : lane + 128] = high
                        spec_low[b, pl.ds(at, 32), lane : lane + 128] = low

            for b in range(banks):
                product = jnp.dot(taps_band[b], spec_high[b], preferred_element_type=f32)
                rest = jnp.dot(taps_band[b, :TILE], spec_low[b], preferred_element_type=f32)
                moved[b] = product[:TILE] + product[TILE:] + rest

            @pl.loop(0, TILE // 32)
            def _(step):
                at = pl.multiple_of(step * 32, 32)
                rate = rate_ref[pl.ds(start + at, 32)]
                for lane in range(0, width, 128):
                    lanes = pl.ds(pl.multiple_of(offset + lane, 128), 128)
                    values = []
                    for b in range(banks):
                        wave = cosine_turns(rate * base_ref[b : b + 1, lanes] - quarter)
                        crossed = pltpu.roll(wave, HALF, 1)
                        value = moved[b, pl.ds(at, 32), lane : lane + 128]
                        values.append(
                            value * jnp.where(left, wave, crossed)
                            + pltpu.roll(value, HALF, 1) * jnp.where(left, -crossed, wave)
                        )
                    for a, value in enumerate(butterfly(values, 1, turn_lanes)):
                        folded[a, pl.ds(start + at, 32), lanes] = value.astype(bf16)

        for distance in range(1, banks):
            backward(chunk, distance).start()
        own_back(chunk).start()

    @pl.when(has_previous)
    def _():
        for piece in range(reach):
            rim(piece).wait_send()
        edge().wait_send()

    @pl.when(has_next)
    def _():
        for piece in range(max(chunks - 1, 0), reach):
            rim(piece).wait_recv()

    @pl.loop(0, chunks)
    def _(chunk):
        for distance in range(1, banks):
            outward(chunk, distance).wait_send()
            backward(chunk, distance).wait()
        own_back(chunk).wait()


def focus_call(echo, code, twist, high, low, offsets, weights, rate, base, banks):
    first, second = twist.shape[1:]
    rows = echo.shape[1]
    chunks = rows // TILE
    span = code.shape[2]
    reach = span // TILE - 1
    lanes = first * 128
    width = min(256, lanes)
    vmem = pl.BlockSpec(memory_space=pltpu.VMEM)
    dma = pltpu.SemaphoreType.DMA
    return pl.pallas_call(
        functools.partial(focus_kernel, banks, first, second, weights.shape[2]),
        in_specs=[pl.BlockSpec(memory_space=pl.ANY), vmem, vmem, vmem, vmem, pl.BlockSpec(memory_space=pltpu.SMEM), vmem, vmem, vmem],
        out_specs=pl.BlockSpec(memory_space=pl.ANY),
        out_shape=jax.ShapeDtypeStruct((banks, rows, lanes), bf16),
        scratch_shapes=[
            pltpu.VMEM((2, rows, first * second), f32),
            pltpu.VMEM((2, rows + reach * TILE, first * second), bf16),
            pltpu.VMEM((4 * TILE, 2 * span), bf16),
            pltpu.VMEM((first, 2, TILE, second), f32),
            pltpu.VMEM((first * TILE, 2 * second), bf16),
            pltpu.VMEM((first * TILE, 2 * second), bf16),
            pltpu.VMEM((first * TILE, 2 * second), f32),
            pltpu.VMEM((banks, rows, lanes), bf16),
            pltpu.VMEM((banks, rows + RIM_ROWS, lanes), bf16),
            pltpu.VMEM((banks, 2 * TILE, TILE + RIM_ROWS), bf16),
            pltpu.VMEM((banks, TILE + RIM_ROWS, width), bf16),
            pltpu.VMEM((banks, TILE + RIM_ROWS, width), bf16),
            pltpu.VMEM((banks, TILE, width), f32),
            pltpu.VMEM((banks, rows, lanes), bf16),
            dma((chunks,)),
            dma((reach,)),
            dma((reach,)),
            dma((chunks, banks - 1)),
            dma((chunks, banks - 1)),
            dma,
            dma,
            dma((chunks, banks - 1)),
            dma((chunks, banks - 1)),
            dma((chunks,)),
        ],
        compiler_params=pltpu.CompilerParams(vmem_limit_bytes=VMEM_LIMIT, collective_id=0, has_side_effects=True),
        cost_estimate=pl.CostEstimate(flops=rows * 34_000_000, bytes_accessed=rows * 30_000, transcendentals=0),
        name="focus",
    )(echo, code, twist, high, low, offsets, weights, rate, base)


def inverse_kernel(first, second, banks, in_ref, twist_ref, high_ref, low_ref, *refs):
    out_ref, gathered, turned = refs[-3:]
    for k in range(first):
        for g in range(banks):
            gathered[k * TILE : (k + 1) * TILE, g * 128 : (g + 1) * 128] = in_ref[g, :, k * 128 : (k + 1) * 128]
    value = gathered[...]
    across = (((1,), (1,)), ((), ()))
    turned[...] = lax.dot_general(value, high_ref[...], across, preferred_element_type=f32) + lax.dot_general(
        value, low_ref[...], across, preferred_element_type=f32
    )

    @pl.loop(0, TILE // 16)
    def _(chunk):
        at = pl.multiple_of(chunk * 16, 16)
        for lane in range(0, second, 128):
            values = []
            for k in range(first):
                where = pl.ds(pl.multiple_of(k * TILE + at, 16), 16)
                re = turned[where, lane : lane + 128]
                im = turned[where, second + lane : second + lane + 128]
                c = twist_ref[0, k : k + 1, lane : lane + 128]
                s = twist_ref[1, k : k + 1, lane : lane + 128]
                values.append((re * c - im * s, im * c + re * s))
            for a, (re, im) in enumerate(butterfly(values, 1, turn_pair)):
                lanes = slice(a * second + lane, a * second + lane + 128)
                out_ref[0, pl.ds(at, 16), lanes] = re
                out_ref[1, pl.ds(at, 16), lanes] = im


def inverse_call(previous, received, twist, high, low, start, total_rows):
    banks, rows, lanes = received.shape
    first, second = twist.shape[1:]
    whole = lambda shape: pl.BlockSpec(shape, lambda s: (0,) * len(shape))
    specs = [pl.BlockSpec((banks, TILE, lanes), lambda s: (0, s, 0)), whole(twist.shape), whole(high.shape), whole(low.shape)]
    operands = [received, twist, high, low]
    aliases = {}
    if previous is not None:
        specs.append(pl.BlockSpec(memory_space=pl.ANY))
        operands.append(previous)
        aliases = {4: 0}
    return pl.pallas_call(
        functools.partial(inverse_kernel, first, second, banks),
        grid=(rows // TILE,),
        in_specs=specs,
        out_specs=pl.BlockSpec((2, TILE, first * second), lambda s: (0, start // TILE + s, 0)),
        out_shape=jax.ShapeDtypeStruct((2, total_rows, first * second), f32),
        scratch_shapes=[
            pltpu.VMEM((first * TILE, 2 * second), bf16),
            pltpu.VMEM((first * TILE, 2 * second), f32),
        ],
        input_output_aliases=aliases,
        compiler_params=pltpu.CompilerParams(vmem_limit_bytes=VMEM_LIMIT),
        cost_estimate=pl.CostEstimate(flops=rows * 10_000_000, bytes_accessed=rows * 30_000, transcendentals=0),
        name="inverse",
    )(*operands)


def tables(banks, first, second):
    pulses = banks * first * second
    inner = np.arange(second)
    highs, lows, twists = [], [], []
    for bank in range(banks):
        steps = banks * inner + bank
        angle = 2.0 * np.pi * ((steps[:, None] * inner[None, :]) % (banks * second)) / (banks * second)
        c, s = np.cos(angle), np.sin(angle)
        re_out = np.concatenate([c, s], axis=0).reshape(2 * second, banks, HALF)
        im_out = np.concatenate([-s, c], axis=0).reshape(2 * second, banks, HALF)
        table = np.stack([re_out, im_out], axis=2).reshape(2 * second, 2 * second)
        high = table.astype(ml_dtypes.bfloat16)
        highs.append(high)
        lows.append((table - high.astype(np.float64)).astype(ml_dtypes.bfloat16))
        angle = 2.0 * np.pi * ((np.arange(first)[:, None] * steps[None, :]) % pulses) / pulses
        twists.append(np.stack([np.cos(angle), np.sin(angle)]).astype(np.float32))
    return np.stack(highs), np.stack(lows), np.stack(twists)


def local(echo_planes, pulse_phase, band_offsets, band_weights, azimuth_rate):
    banks = lax.axis_size("az")
    bank = lax.axis_index("az")
    row_count, pulse_local = echo_planes.shape[1:]
    pulse_count = pulse_local * banks
    second = HALF * banks
    first = pulse_local // second
    code_length = pulse_phase.shape[0]
    reach = -(-code_length // TILE)
    highs, lows, twists = tables(banks, first, second)
    pick = lambda stack: lax.dynamic_index_in_dim(jnp.asarray(stack), bank, 0, keepdims=False)
    high, low, twist = pick(highs), pick(lows), pick(twists)
    span = (reach + 1) * TILE
    norm_scale = 1.0 / math.sqrt(code_length)
    code = jnp.stack([jnp.cos(pulse_phase), jnp.sin(pulse_phase)]) * norm_scale
    code = jnp.pad(code, ((0, 0), (0, span - code_length)))[:, None, :]

    offsets = band_offsets[:, 0, 0]
    weights = band_weights[:, 0].transpose(0, 2, 1)
    rate = jnp.broadcast_to(azimuth_rate[:, None], (row_count, 128))
    lane = jnp.arange(first * 128, dtype=jnp.int32)
    bins = bank * (HALF * first) + first * (lane % HALF) + lane // 128
    bins = bins[None, :] + pulse_local * jnp.arange(banks, dtype=jnp.int32)[:, None]
    centered = jnp.where(bins < pulse_count // 2, bins, bins - pulse_count)
    frequency = centered.astype(f32) / pulse_count
    base = 0.5 * frequency * frequency

    received = focus_call(echo_planes, code, twist, high, low, offsets, weights, rate, base, banks)
    return inverse_call(None, received, twist * (1.0 / pulse_count), high, low, 0, row_count)


def solution(mesh):
    in_specs = (P(None, "rg", "az"), P(), P(None, "az", "rg"), P(None, "az", None, "rg"), P("rg"))
    out_specs = P(None, "rg", "az")
    return jax.shard_map(local, mesh=mesh, in_specs=in_specs, out_specs=out_specs, check_vma=False)
```

time: 277 us -> 216 us (0.78)
  the two profiles are of different devices: /device:TPU:2 before, /device:TPU:14 now
where the time goes in v2:
time: 216 us; the launch traced here: 215 us
  Pallas kernels  205 us (95%)
  local copies, waits for them, and re-layouts  7.76 us (4%)
    pallas_call x1, Pallas kernels, focus_call(): pl.pallas_call(functools.partial(focus_kernel, banks, first, second, weig...  195 us
    pallas_call x1, Pallas kernels, inverse_call(): pl.pallas_call(functools.partial(inverse_kernel, first, second, banks), g...  10.5 us

profile of v2, /device:TPU:14, one launch (start us, length us, event | category | flops | bytes accessed | tf_op | source)
XLA Modules:
  0.0 215.2 jit_solution(17637992261451037718)
XLA Ops:
  0.0 0.0 copy-start
  0.0 0.8 fusion.10
  0.8 0.6 broadcast_in_dim.4.code_ref
  1.4 0.7 multiply_multiply_fusion.base_ref
  2.1 1.3 broadcast_multiply_fusion.twist_ref
  3.4 1.3 dynamic-slice_bitcast_fusion.2.twist_ref
  4.7 1.5 broadcast_in_dim.5.rate_ref
  6.3 2.2 %dynamic-slice_bitcast_fusion = (bf16[512,512]{1,0:T(8,128)(2,1)}, bf16[512,512]{1,0:T(8,128)(2,1)}) fusion(bf16[4,512,512]{2,1,0:T(8,128)(2,1)} %constant.79.clone, s32[]{:T(128)S(6)} %select_n.31, bf16[4,512,512]{2,1,0:T(8,128)(2,1)} %constant.78.clone), kind=kLoop, calls=%fused_computation | loop fusion | bytes 2097156 | tf_op jit(solution)/shard_map/jit(dynamic_index_in_dim)/squeeze | solution.py:456
  8.5 0.0 copy-done
  8.5 1.3 copy.9
  9.8 194.9 %focus.1.in_ref = bf16[4,512,1024]{2,1,0:T(8,128)(2,1)} custom-call(f32[2,512,2048]{2,1,0:T(8,128)} %echo_ref.1, f32[2,1,512]{2,1,0:T(1,128)} %broadcast_in_dim.4.code_ref, f32[2,8,256]{2,1,0:T(8,128)} %dynamic-slice_bitcast_fusion.2.twist_ref, bf16[512,512]{1,0:T(8,128)(2,1)} %get-tuple-element.8.high_ref, bf16[512,512]{1,0:T(8,128)(2,1)} %get-tuple-element.7.low_ref, ...), custom_call_target="tpu_custom_call" | custom-call | flops 17408000000 | bytes 15360000 | tf_op jit(solution)/shard_map/focus/pallas_call | solution.py:333
  204.7 10.5 %inverse.1 = f32[2,512,2048]{2,1,0:T(8,128)} custom-call(bf16[4,512,1024]{2,1,0:T(8,128)(2,1)} %focus.1.in_ref, f32[2,8,256]{2,1,0:T(8,128)} %broadcast_multiply_fusion.twist_ref, bf16[512,512]{1,0:T(8,128)(2,1)} %get-tuple-element.8.high_ref, bf16[512,512]{1,0:T(8,128)(2,1)} %get-tuple-element.7.low_ref), custom_call_target="tpu_custom_call" | custom-call | flops 5120000000 | bytes 15360000 | tf_op jit(solution)/shard_map/inverse/pallas_call | solution.py:410
  (6 shorter events, 0.0 us)
Async XLA Ops:
  0.0 8.5 %copy-start = (f32[4,1,8,512]{3,2,1,0:T(8,128)S(1)}, f32[4,1,8,512]{3,2,1,0:T(8,128)}, u32[]{:S(2)}) copy-start(f32[4,1,8,512]{3,2,1,0:T(8,128)} %param.11) | copy-start | bytes 196612

commit v3 on v2

--- a/solution.py
+++ b/solution.py
@@ -64,16 +64,18 @@
 
 
 def focus_kernel(
-    banks, first, second, taps, echo_ref, code_ref, twist_ref, high_ref, low_ref, offset_ref, weight_ref, rate_ref, base_ref, out_ref,
+    banks, first, second, taps, echo_ref, phase_ref, twist_all, high_all, low_all, offset_ref, weight_ref, rate_all, out_ref,
     stage, window, band, comp, spread_high, spread_low, result, send, spectra, taps_band, spec_high, spec_low, moved, folded,
-    load_sem, rim_send, rim_recv, out_send, out_recv, edge_send, edge_recv, back_send, back_recv, own_sem,
+    high_ref, low_ref, rate_ref, base_ref, load_sem, table_sem, rim_send, rim_recv, out_send, out_recv, edge_send, edge_recv, back_send, back_recv, own_sem,
 ):
     bank, block = lax.axis_index("az"), lax.axis_index("rg")
     block_count = lax.axis_size("rg")
     rows = echo_ref.shape[1]
     chunks = rows // TILE
-    span = code_ref.shape[2]
-    reach = span // TILE - 1
+    code_length = phase_ref.shape[1]
+    reach = -(-code_length // TILE)
+    span = (reach + 1) * TILE
+    twist_ref = twist_all.at[bank]
     width = min(256, first * 128)
     wide = TILE + RIM_ROWS
     has_next = block < block_count - 1
@@ -123,6 +125,12 @@
 
     for chunk in range(chunks):
         load(chunk).start()
+    table_copies = [
+        pltpu.make_async_copy(source.at[bank], target, table_sem.at[index])
+        for index, (source, target) in enumerate(((high_all, high_ref), (low_all, low_ref)))
+    ]
+    for copy in table_copies:
+        copy.start()
 
     barrier = pltpu.get_barrier_semaphore()
     for distance in range(1, banks):
@@ -138,29 +146,10 @@
     def _():
         pl.semaphore_signal(barrier, inc=1, device_id={"rg": block + 1}, device_id_type=pl.DeviceIdType.MESH)
 
-    pl.semaphore_wait(barrier, banks - 1 + has_previous.astype(jnp.int32) + has_next.astype(jnp.int32))
-
-    for chunk in range(chunks):
-        load(chunk).wait()
-
-        @pl.loop(0, TILE // 16)
-        def _(step):
-            at = pl.ds(pl.multiple_of(chunk * TILE + step * 16, 16), 16)
-            window[:, at] = stage[:, at].astype(bf16)
-
-        if chunk < reach:
-
-            @pl.when(has_previous)
-            def _():
-                rim(chunk).start()
-
-    @pl.when(jnp.logical_not(has_next))
-    def _():
-        window[:, rows : rows + reach * TILE] = jnp.zeros((2, reach * TILE, first * second), bf16)
-        spectra[:, rows : rows + RIM_ROWS] = jnp.zeros((banks, RIM_ROWS, first * 128), bf16)
-
     def shifted(index):
-        whole = jnp.broadcast_to(code_ref[index], (TILE, span))
+        row = (jnp.cos, jnp.sin)[index](phase_ref[...]) * (1.0 / math.sqrt(code_length))
+        row = jnp.concatenate([row, jnp.zeros((1, span - code_length), f32)], axis=1)
+        whole = jnp.broadcast_to(row, (TILE, span))
         return split(pltpu.roll(whole, 0, 1, stride=1, stride_axis=0))
 
     for part, (c, s) in enumerate(zip(shifted(0), shifted(1))):
@@ -169,6 +158,39 @@
         band[at : at + TILE, span:] = s
         band[at + TILE : at + 2 * TILE, :span] = -s
         band[at + TILE : at + 2 * TILE, span:] = c
+
+    lane_id = lax.broadcasted_iota(jnp.int32, (1, 128), 1)
+    pulse_local, pulse_count = first * second, banks * first * second
+    for k in range(first):
+        for b in range(banks):
+            bins = bank * (HALF * first) + first * (lane_id % HALF) + (k + pulse_local * b)
+            centered = jnp.where(bins < pulse_count // 2, bins, bins - pulse_count)
+            frequency = centered.astype(f32) * (1.0 / pulse_count)
+            base_ref[b : b + 1, k * 128 : (k + 1) * 128] = 0.5 * frequency * frequency
+
+    pl.semaphore_wait(barrier, banks - 1 + has_previous.astype(jnp.int32) + has_next.astype(jnp.int32))
+
+    for chunk in range(chunks):
+        load(chunk).wait()
+
+        @pl.loop(0, TILE // 16)
+        def _(step):
+            at = pl.ds(pl.multiple_of(chunk * TILE + step * 16, 16), 16)
+            window[:, at] = stage[:, at].astype(bf16)
+
+        if chunk < reach:
+
+            @pl.when(has_previous)
+            def _():
+                rim(chunk).start()
+
+    @pl.when(jnp.logical_not(has_next))
+    def _():
+        window[:, rows : rows + reach * TILE] = jnp.zeros((2, reach * TILE, first * second), bf16)
+        spectra[:, rows : rows + RIM_ROWS] = jnp.zeros((banks, RIM_ROWS, first * 128), bf16)
+
+    for copy in table_copies:
+        copy.wait()
 
     @pl.loop(0, chunks)
     def _(chunk):
@@ -246,7 +268,9 @@
         def _():
             edge().wait_recv()
 
+        rate_ref[...] = jnp.broadcast_to(rate_all[:, pl.ds(start, TILE)], (128, TILE)).T
         for b in range(banks):
+            turned = weight_ref[b, 0, :, pl.ds(start, TILE)].T
             steps = (
                 lax.broadcasted_iota(jnp.int32, (TILE, wide), 1)
                 - lax.broadcasted_iota(jnp.int32, (TILE, wide), 0)
@@ -254,7 +278,7 @@
             )
             total = jnp.zeros((TILE, wide), f32)
             for t in range(taps):
-                total = jnp.where(steps == t, weight_ref[b, pl.ds(start, TILE), t : t + 1], total)
+                total = jnp.where(steps == t, turned[:, t : t + 1], total)
             high, low = split(total)
             taps_band[b, :TILE] = high
             taps_band[b, TILE:] = low
@@ -282,7 +306,7 @@
             @pl.loop(0, TILE // 32)
             def _(step):
                 at = pl.multiple_of(step * 32, 32)
-                rate = rate_ref[pl.ds(start + at, 32)]
+                rate = rate_ref[pl.ds(at, 32)]
                 for lane in range(0, width, 128):
                     lanes = pl.ds(pl.multiple_of(offset + lane, 128), 128)
                     values = []
@@ -320,19 +344,20 @@
         own_back(chunk).wait()
 
 
-def focus_call(echo, code, twist, high, low, offsets, weights, rate, base, banks):
-    first, second = twist.shape[1:]
+def focus_call(echo, phase, twist, high, low, offsets, weights, rate, banks):
+    first, second = twist.shape[2:]
     rows = echo.shape[1]
     chunks = rows // TILE
-    span = code.shape[2]
-    reach = span // TILE - 1
+    reach = -(-phase.shape[1] // TILE)
+    span = (reach + 1) * TILE
     lanes = first * 128
     width = min(256, lanes)
     vmem = pl.BlockSpec(memory_space=pltpu.VMEM)
+    anywhere = pl.BlockSpec(memory_space=pl.ANY)
     dma = pltpu.SemaphoreType.DMA
     return pl.pallas_call(
         functools.partial(focus_kernel, banks, first, second, weights.shape[2]),
-        in_specs=[pl.BlockSpec(memory_space=pl.ANY), vmem, vmem, vmem, vmem, pl.BlockSpec(memory_space=pltpu.SMEM), vmem, vmem, vmem],
+        in_specs=[anywhere, vmem, vmem, anywhere, anywhere, pl.BlockSpec(memory_space=pltpu.SMEM), vmem, vmem],
         out_specs=pl.BlockSpec(memory_space=pl.ANY),
         out_shape=jax.ShapeDtypeStruct((banks, rows, lanes), bf16),
         scratch_shapes=[
@@ -350,7 +375,12 @@
             pltpu.VMEM((banks, TILE + RIM_ROWS, width), bf16),
             pltpu.VMEM((banks, TILE, width), f32),
             pltpu.VMEM((banks, rows, lanes), bf16),
+            pltpu.VMEM((2 * second, 2 * second), bf16),
+            pltpu.VMEM((2 * second, 2 * second), bf16),
+            pltpu.VMEM((TILE, 128), f32),
+            pltpu.VMEM((banks, lanes), f32),
             dma((chunks,)),
+            dma((2,)),
             dma((reach,)),
             dma((reach,)),
             dma((chunks, banks - 1)),
@@ -364,11 +394,25 @@
         compiler_params=pltpu.CompilerParams(vmem_limit_bytes=VMEM_LIMIT, collective_id=0, has_side_effects=True),
         cost_estimate=pl.CostEstimate(flops=rows * 34_000_000, bytes_accessed=rows * 30_000, transcendentals=0),
         name="focus",
-    )(echo, code, twist, high, low, offsets, weights, rate, base)
-
-
-def inverse_kernel(first, second, banks, in_ref, twist_ref, high_ref, low_ref, *refs):
-    out_ref, gathered, turned = refs[-3:]
+    )(echo, phase, twist, high, low, offsets, weights, rate)
+
+
+def inverse_kernel(first, second, banks, in_ref, twist_all, high_all, low_all, out_ref, gathered, turned, high_ref, low_ref, table_sem):
+    bank = lax.axis_index("az")
+    twist_ref = twist_all.at[bank]
+    scale = 1.0 / (banks * first * second)
+
+    @pl.when(pl.program_id(0) == 0)
+    def _():
+        copies = [
+            pltpu.make_async_copy(source.at[bank], target, table_sem.at[index])
+            for index, (source, target) in enumerate(((high_all, high_ref), (low_all, low_ref)))
+        ]
+        for copy in copies:
+            copy.start()
+        for copy in copies:
+            copy.wait()
+
     for k in range(first):
         for g in range(banks):
             gathered[k * TILE : (k + 1) * TILE, g * 128 : (g + 1) * 128] = in_ref[g, :, k * 128 : (k + 1) * 128]
@@ -387,8 +431,8 @@
                 where = pl.ds(pl.multiple_of(k * TILE + at, 16), 16)
                 re = turned[where, lane : lane + 128]
                 im = turned[where, second + lane : second + lane + 128]
-                c = twist_ref[0, k : k + 1, lane : lane + 128]
-                s = twist_ref[1, k : k + 1, lane : lane + 128]
+                c = twist_ref[0, k : k + 1, lane : lane + 128] * scale
+                s = twist_ref[1, k : k + 1, lane : lane + 128] * scale
                 values.append((re * c - im * s, im * c + re * s))
             for a, (re, im) in enumerate(butterfly(values, 1, turn_pair)):
                 lanes = slice(a * second + lane, a * second + lane + 128)
@@ -396,32 +440,33 @@
                 out_ref[1, pl.ds(at, 16), lanes] = im
 
 
-def inverse_call(previous, received, twist, high, low, start, total_rows):
+def inverse_call(received, twist, high, low):
     banks, rows, lanes = received.shape
-    first, second = twist.shape[1:]
-    whole = lambda shape: pl.BlockSpec(shape, lambda s: (0,) * len(shape))
-    specs = [pl.BlockSpec((banks, TILE, lanes), lambda s: (0, s, 0)), whole(twist.shape), whole(high.shape), whole(low.shape)]
-    operands = [received, twist, high, low]
-    aliases = {}
-    if previous is not None:
-        specs.append(pl.BlockSpec(memory_space=pl.ANY))
-        operands.append(previous)
-        aliases = {4: 0}
+    first, second = twist.shape[2:]
+    anywhere = pl.BlockSpec(memory_space=pl.ANY)
+    specs = [
+        pl.BlockSpec((banks, TILE, lanes), lambda s: (0, s, 0)),
+        pl.BlockSpec(twist.shape, lambda s: (0, 0, 0, 0)),
+        anywhere,
+        anywhere,
+    ]
     return pl.pallas_call(
         functools.partial(inverse_kernel, first, second, banks),
         grid=(rows // TILE,),
         in_specs=specs,
-        out_specs=pl.BlockSpec((2, TILE, first * second), lambda s: (0, start // TILE + s, 0)),
-        out_shape=jax.ShapeDtypeStruct((2, total_rows, first * second), f32),
+        out_specs=pl.BlockSpec((2, TILE, first * second), lambda s: (0, s, 0)),
+        out_shape=jax.ShapeDtypeStruct((2, rows, first * second), f32),
         scratch_shapes=[
             pltpu.VMEM((first * TILE, 2 * second), bf16),
             pltpu.VMEM((first * TILE, 2 * second), f32),
+            pltpu.VMEM((2 * second, 2 * second), bf16),
+            pltpu.VMEM((2 * second, 2 * second), bf16),
+            pltpu.SemaphoreType.DMA((2,)),
         ],
-        input_output_aliases=aliases,
         compiler_params=pltpu.CompilerParams(vmem_limit_bytes=VMEM_LIMIT),
         cost_estimate=pl.CostEstimate(flops=rows * 10_000_000, bytes_accessed=rows * 30_000, transcendentals=0),
         name="inverse",
-    )(*operands)
+    )(received, twist, high, low)
 
 
 def tables(banks, first, second):
@@ -445,33 +490,12 @@
 
 def local(echo_planes, pulse_phase, band_offsets, band_weights, azimuth_rate):
     banks = lax.axis_size("az")
-    bank = lax.axis_index("az")
-    row_count, pulse_local = echo_planes.shape[1:]
-    pulse_count = pulse_local * banks
     second = HALF * banks
-    first = pulse_local // second
-    code_length = pulse_phase.shape[0]
-    reach = -(-code_length // TILE)
-    highs, lows, twists = tables(banks, first, second)
-    pick = lambda stack: lax.dynamic_index_in_dim(jnp.asarray(stack), bank, 0, keepdims=False)
-    high, low, twist = pick(highs), pick(lows), pick(twists)
-    span = (reach + 1) * TILE
-    norm_scale = 1.0 / math.sqrt(code_length)
-    code = jnp.stack([jnp.cos(pulse_phase), jnp.sin(pulse_phase)]) * norm_scale
-    code = jnp.pad(code, ((0, 0), (0, span - code_length)))[:, None, :]
-
-    offsets = band_offsets[:, 0, 0]
-    weights = band_weights[:, 0].transpose(0, 2, 1)
-    rate = jnp.broadcast_to(azimuth_rate[:, None], (row_count, 128))
-    lane = jnp.arange(first * 128, dtype=jnp.int32)
-    bins = bank * (HALF * first) + first * (lane % HALF) + lane // 128
-    bins = bins[None, :] + pulse_local * jnp.arange(banks, dtype=jnp.int32)[:, None]
-    centered = jnp.where(bins < pulse_count // 2, bins, bins - pulse_count)
-    frequency = centered.astype(f32) / pulse_count
-    base = 0.5 * frequency * frequency
-
-    received = focus_call(echo_planes, code, twist, high, low, offsets, weights, rate, base, banks)
-    return inverse_call(None, received, twist * (1.0 / pulse_count), high, low, 0, row_count)
+    high, low, twist = (jnp.asarray(table) for table in tables(banks, echo_planes.shape[2] // second, second))
+    received = focus_call(
+        echo_planes, pulse_phase[None], twist, high, low, band_offsets[:, 0, 0], band_weights, azimuth_rate[None], banks
+    )
+    return inverse_call(received, twist, high, low)
 
 
 def solution(mesh):

time: 216 us -> 207 us (0.958)
  local copies, waits for them, and re-layouts: 7.76 us -> 1.24 us
    squeeze x2 -> x0, local copies, waits for them, and re-layouts: 3.56 us -> none  [local(): lax.dynamic_index_in_dim(jnp.asarray(stack), bank, 0, keepdims=False)]
where the time goes in v3:
time: 207 us
  Pallas kernels  206 us (100%)
    pallas_call x1, Pallas kernels, focus_call(): pl.pallas_call(functools.partial(focus_kernel, banks, first, second, weig...  194 us
    pallas_call x1, Pallas kernels, inverse_call(): pl.pallas_call(functools.partial(inverse_kernel, first, second, banks), g...  11.7 us

profile of v3, /device:TPU:14, one launch (start us, length us, event | category | flops | bytes accessed | tf_op | source)
XLA Modules:
  0.0 207.0 jit_solution(7074369414915304320)
XLA Ops:
  0.0 1.2 broadcast_in_dim.6.phase_ref
  1.2 194.0 %focus.1.in_ref = bf16[4,512,1024]{2,1,0:T(8,128)(2,1)} custom-call(f32[2,512,2048]{2,1,0:T(8,128)} %echo_ref.1, f32[1,384]{1,0:T(1,128)} %broadcast_in_dim.6.phase_ref, f32[4,2,8,256]{3,2,1,0:T(8,128)} %constant.8.clone.twist_all, bf16[4,512,512]{2,1,0:T(8,128)(2,1)} %constant.6.clone.high_all, bf16[4,512,512]{2,1,0:T(8,128)(2,1)} %constant.7.clone.low_all, ...), custom_call_target="tpu_custom_call" | custom-call | flops 17408000000 | bytes 15360000 | tf_op jit(solution)/shard_map/focus/pallas_call | solution.py:358
  195.3 11.7 %inverse.1 = f32[2,512,2048]{2,1,0:T(8,128)} custom-call(bf16[4,512,1024]{2,1,0:T(8,128)(2,1)} %focus.1.in_ref, f32[4,2,8,256]{3,2,1,0:T(8,128)} %constant.8.clone.twist_all, bf16[4,512,512]{2,1,0:T(8,128)(2,1)} %constant.6.clone.high_all, bf16[4,512,512]{2,1,0:T(8,128)(2,1)} %constant.7.clone.low_all), custom_call_target="tpu_custom_call" | custom-call | flops 5120000000 | bytes 15360000 | tf_op jit(solution)/shard_map/inverse/pallas_call | solution.py:453
